TPU v7x, 256 devices: a whole 4x4x8 slice. The times are simulated.
256 devices in a mesh: row: 8 (over y, z_hi), col: 32 (over z_lo, x, core).
Axes of the slice: x: 4, y: 4, z: 8 (z_hi: 2, z_lo: 4; z = z_hi * 4 + z_lo), core: 2. Of those that a mesh axis runs over, the one named last changes fastest.
Arguments:
- region: bfloat16 [128, 1536, 96], P('row', 'col'), may hold values from -6 to 6
- cotangent: bfloat16 [128, 1536, 96], P('row', 'col'), may hold values from -6 to 6
- norm_gains: float32 [2, 2, 96], replicated, may hold values from 0.5 to 1.5
- qkv_weight: bfloat16 [2, 96, 288], replicated, may hold values from -0.625 to 0.625
- qkv_bias: float32 [2, 288], replicated, may hold values from -3 to 3
- bias_table: float32 [2, 3, 225], replicated, may hold values from -4 to 300
- proj_weight: bfloat16 [2, 96, 96], replicated, may hold values from -0.625 to 0.625
- up_weight: bfloat16 [2, 96, 384], replicated, may hold values from -0.625 to 0.625
- up_bias: float32 [2, 384], replicated, may hold values from -3 to 3
- down_weight: bfloat16 [2, 384, 96], replicated, may hold values from -0.3125 to 0.3125
Outputs:
- output: bfloat16 [128, 1536, 96], P('row', 'col')
- grad_region: float32 [128, 1536, 96], P('row', 'col')
- grad_gains: float32 [2, 2, 96], replicated
- grad_qkv_weight: float32 [2, 96, 288], replicated
- grad_qkv_bias: float32 [2, 288], replicated
- grad_table: float32 [2, 3, 225], replicated
- grad_proj: float32 [2, 96, 96], replicated
- grad_up_weight: float32 [2, 96, 384], replicated
- grad_up_bias: float32 [2, 384], replicated
- grad_down_weight: float32 [2, 384, 96], replicated
All inputs are finite; a program needn't handle non-finite values.
Results may differ from a plain program's by a relative error of at most 0.025.
Values may be sent and summed in bfloat16 or wider, within the bound.
No kernel may reach another device: no remote copies, remote signals or barrier semaphores. Data moves between devices by JAX's collectives and lax.ppermute only.
A program may use at most 64 MiB of HBM per device.

v0:
```python
import jax
import jax.numpy as jnp
from jax import lax
from jax.sharding import PartitionSpec as P

WIN = 8


HIGHEST = lax.Precision.HIGHEST


def padded_2(shard, sides, width):
    for axis, dim in sides:
        count, length = (lax.axis_size(axis), shard.shape[dim])
        up = [(i, (i + 1) % count) for i in range(count - 1)]
        down = [(j, i) for i, j in up]
        last = lax.slice_in_dim(shard, length - width, length, axis=dim)
        initial = lax.slice_in_dim(shard, 0, width, axis=dim)
        before = lax.ppermute(last, axis, up)
        after = lax.ppermute(initial, axis, down)
        shard = jnp.concatenate([before, shard, after], axis=dim)
    return shard


def for_sending(shard):
    return jax.tree.map(lambda a: a.astype(jnp.bfloat16) if a.dtype == jnp.float32 else a, shard)


def layer_norm(values, gain):
    average = jnp.mean(values, -1, keepdims=True)
    centred = values - average
    variance = jnp.mean(centred * centred, -1, keepdims=True)
    return centred * lax.rsqrt(variance + 1e-05) * gain


def position_bias(table):
    positions = jnp.arange(WIN * WIN, dtype=jnp.int32)
    pos_row = positions // WIN
    pos_col = positions % WIN
    table_side = 2 * WIN - 1
    table_index = (pos_row[:, None] - pos_row[None, :] + WIN - 1) * table_side + (
        pos_col[:, None] - pos_col[None, :] + WIN - 1
    )
    onehot = (
        table_index[:, :, None]
        == jnp.arange(table_side * table_side, dtype=jnp.int32)[None, None, :]
    ).astype(jnp.float32)
    return jnp.einsum("qkt,ht->hqk", onehot, table, precision=HIGHEST)


def windowize(field):
    height, width, depth = field.shape
    blocks = field.reshape(height // WIN, WIN, width // WIN, WIN, depth)
    return blocks.transpose(0, 2, 1, 3, 4).reshape(-1, WIN * WIN, depth)


def unwindowize(windows, height, width):
    depth = windows.shape[-1]
    blocks = windows.reshape(height // WIN, width // WIN, WIN, WIN, depth)
    return blocks.transpose(0, 2, 1, 3, 4).reshape(height, width, depth)


def attend(windows, usable, layer):
    gain_pair, qkv_weight, qkv_bias, table, proj_weight = layer[:5]
    win_count, win_tokens, channels = windows.shape
    head_count = table.shape[0]
    head_size = channels // head_count
    normed = (
        layer_norm(windows, gain_pair[0])
        .astype(jnp.bfloat16)
        .reshape(win_count * win_tokens, channels)
    )
    triple = (jnp.dot(normed, qkv_weight, preferred_element_type=jnp.float32) + qkv_bias).astype(
        jnp.bfloat16
    )
    triple = triple.reshape(win_count, win_tokens, 3, head_count, head_size)
    queries = triple[:, :, 0]
    key_part = triple[:, :, 1]
    value_part = triple[:, :, 2]
    scores = (
        jnp.einsum("wqhd,wkhd->whqk", queries, key_part, preferred_element_type=jnp.float32)
        * head_size ** (-0.5)
        + position_bias(table)[None]
    )
    if usable is not None:
        scores = jnp.where(usable[:, None, None, :], scores, -1e30)
    highest = lax.stop_gradient(jnp.max(scores, -1, keepdims=True))
    exponent = jnp.exp(scores - highest)
    softmax_w = (exponent / jnp.sum(exponent, -1, keepdims=True)).astype(jnp.bfloat16)
    mixture = jnp.einsum(
        "whqk,wkhd->wqhd", softmax_w, value_part, preferred_element_type=jnp.float32
    ).astype(jnp.bfloat16)
    mixture = mixture.reshape(win_count * win_tokens, channels)
    projected = jnp.dot(mixture, proj_weight, preferred_element_type=jnp.float32)
    return windows + projected.reshape(win_count, win_tokens, channels)


def feed(field, layer):
    gain_pair = layer[0]
    up_weight, up_bias, down_weight = layer[5:]
    channels = field.shape[-1]
    flat_rows = field.reshape(-1, channels)
    normed = layer_norm(flat_rows, gain_pair[1]).astype(jnp.bfloat16)
    hidden = jax.nn.gelu(
        jnp.dot(normed, up_weight, preferred_element_type=jnp.float32) + up_bias
    ).astype(jnp.bfloat16)
    return (flat_rows + jnp.dot(hidden, down_weight, preferred_element_type=jnp.float32)).reshape(
        field.shape
    )


def regular(field, layer):
    height, width, _ = field.shape
    return feed(unwindowize(attend(windowize(field), None, layer), height, width), layer)


def shifted(padded, row_start, col_start, total_rows, total_cols, layer):
    half_win = WIN // 2
    height = padded.shape[0] - WIN
    width = padded.shape[1] - WIN
    row_ids = row_start + jnp.arange(height + WIN, dtype=jnp.int32)
    col_ids = col_start + jnp.arange(width + WIN, dtype=jnp.int32)
    inside = ((row_ids >= 0) & (row_ids < total_rows))[:, None] & (
        (col_ids >= 0) & (col_ids < total_cols)
    )[None, :]
    usable = windowize(inside[:, :, None]).reshape(-1, WIN * WIN)
    mixed_field = unwindowize(attend(windowize(padded), usable, layer), height + WIN, width + WIN)
    return feed(mixed_field[half_win : half_win + height, half_win : half_win + width], layer)


def edge_strips(gradient, dim):
    half_win = WIN // 2
    length = gradient.shape[dim]
    head_strip = lax.slice_in_dim(gradient, 0, half_win, axis=dim)
    tail_strip = lax.slice_in_dim(gradient, length - half_win, length, axis=dim)
    return jnp.concatenate([head_strip, tail_strip], dim)


def fold_edges(gradient, widened, dim):
    half_win = WIN // 2
    length = gradient.shape[dim]
    interior = lax.slice_in_dim(gradient, half_win, length - half_win, axis=dim)
    from_lower = lax.slice_in_dim(widened, 0, half_win, axis=dim)
    from_upper = lax.slice_in_dim(widened, 3 * half_win, 4 * half_win, axis=dim)
    inner_len = length - 2 * half_win
    widths_low = [(0, 0)] * gradient.ndim
    widths_low[dim] = (0, inner_len - half_win)
    widths_high = [(0, 0)] * gradient.ndim
    widths_high[dim] = (inner_len - half_win, 0)
    return interior + jnp.pad(from_lower, widths_low) + jnp.pad(from_upper, widths_high)


def flatten(parts):
    return jnp.concatenate([part.astype(jnp.float32).reshape(-1) for part in parts])


def unflatten(flat_vec, shapes_like):
    pieces = []
    offset = 0
    for like in shapes_like:
        length = like.size
        pieces.append(flat_vec[offset : offset + length].reshape(like.shape))
        offset = offset + length
    return pieces


def body(
    region,
    cotangent,
    norm_gains,
    qkv_weight,
    qkv_bias,
    bias_table,
    proj_weight,
    up_weight,
    up_bias,
    down_weight,
):
    stacked = (
        norm_gains,
        qkv_weight,
        qkv_bias,
        bias_table,
        proj_weight,
        up_weight,
        up_bias,
        down_weight,
    )
    lower_layer = tuple((entry[0] for entry in stacked))
    upper_layer = tuple((entry[1] for entry in stacked))
    half_win = WIN // 2
    tile_rows, tile_cols, channels = region.shape
    total_rows = tile_rows * lax.axis_size("row")
    total_cols = tile_cols * lax.axis_size("col")
    row_start = lax.axis_index("row") * tile_rows - half_win
    col_start = lax.axis_index("col") * tile_cols - half_win
    lower_out, pull_lower = jax.vjp(regular, region.astype(jnp.float32), lower_layer)
    lower_bf = lower_out.astype(jnp.bfloat16)
    padded = padded_2(lower_bf, (("row", 0), ("col", 1)), half_win)

    def upper_block(field, layer):
        return shifted(field, row_start, col_start, total_rows, total_cols, layer)

    upper_out, pull_upper = jax.vjp(upper_block, padded.astype(jnp.float32), upper_layer)
    grad_padded, grad_upper = pull_upper(cotangent.astype(jnp.float32))
    upper_flat = flatten(grad_upper)
    widened = padded_2(
        edge_strips(grad_padded, 1).astype(jnp.bfloat16), (("col", 1),), half_win
    ).astype(jnp.float32)
    partial_grad = fold_edges(grad_padded, widened, 1)
    widened = padded_2(for_sending(edge_strips(partial_grad, 0)), (("row", 0),), half_win)
    grad_lower = fold_edges(partial_grad, widened, 0)
    grad_region, grad_lower_layer = pull_lower(grad_lower)
    lower_flat = flatten(grad_lower_layer)
    lower_total, upper_total = lax.psum((lower_flat, upper_flat), ("row", "col"))
    lower_parts = unflatten(lower_total, lower_layer)
    upper_parts = unflatten(upper_total, upper_layer)
    grads = [jnp.stack([low_part, up_part]) for low_part, up_part in zip(lower_parts, upper_parts)]
    return (
        upper_out.astype(jnp.bfloat16),
        grad_region,
        grads[0],
        grads[1],
        grads[2],
        grads[3],
        grads[4],
        grads[5],
        grads[6],
        grads[7],
    )


def solution(mesh):
    return jax.shard_map(
        body,
        mesh=mesh,
        in_specs=(
            P("row", "col", None),
            P("row", "col", None),
            P(),
            P(),
            P(),
            P(),
            P(),
            P(),
            P(),
            P(),
        ),
        out_specs=(
            P("row", "col", None),
            P("row", "col", None),
            P(),
            P(),
            P(),
            P(),
            P(),
            P(),
            P(),
            P(),
        ),
        check_vma=False,
    )
```

profile of v0, /device:TPU:1, one launch (start us, length us, event | category | flops | bytes accessed | tf_op | source)
XLA Modules:
  0.0 455.6 jit_solution(8696084571514175872)
XLA Ops:
  13.7 2.8 fusion.69
  25.9 10.3 %collective-permute-start = (bf16[4,48,96]{2,1,0:T(8,128)(2,1)S(1)}, bf16[4,48,96]{2,1,0:T(8,128)(2,1)S(1)}, u32[]{:S(2)}, u32[]{:S(2)}) collective-permute-start(bf16[4,48,96]{2,1,0:T(8,128)(2,1)S(1)} %bitcast.372), channel_id=1, source_target_pairs={{0,32},{32,64},{64,96},{96,128},{128,160},{160,192},{192,224},{1,3... | collective-permute-start | bytes 110600 | tf_op jit(solution)/shard_map/ppermute | solution.py:19
  36.9 2.8 fusion.70
  39.9 4.0 collective-permute-start.2
  43.9 1.9 collective-permute-start.3
  55.8 1.5 reshape.734
  58.7 2.4 fusion.184
  61.7 1.5 convolution_convert_fusion.7
  66.5 2.0 multiply_convert_fusion.3
  70.1 2.4 fusion.185
  73.7 2.5 fusion.65
  82.2 2.2 reshape.743
  84.4 1.8 fusion.32
  91.8 13.9 %reshape.744 = bf16[1344,288]{0,1:T(8,128)(2,1)S(1)} reshape(bf16[21,64,3,3,32]{1,0,4,3,2:T(8,128)(2,1)S(1)} %copy.219) | data formatting | bytes 1548288 | tf_op jit(solution)/shard_map/transpose(jvp())/reshape | solution.py:76
  105.8 2.1 fusion.74
  114.7 1.8 fusion.77
  121.1 3.6 collective-permute-start.4
  124.8 1.9 collective-permute-start.5
  126.7 1.4 fusion.82
  128.2 1.8 collective-permute-done.5
  130.2 8.6 %collective-permute-start.6 = (bf16[4,48,96]{2,1,0:T(8,128)(2,1)S(1)}, bf16[4,48,96]{2,1,0:T(8,128)(2,1)S(1)}, u32[]{:S(2)}, u32[]{:S(2)}) collective-permute-start(bf16[4,48,96]{2,1,0:T(8,128)(2,1)S(1)} %get-tuple-element.84), channel_id=1, source_target_pairs={{0,32},{32,64},{64,96},{96,128},{128,160},{160,192},{192,224},{1,3... | collective-permute-start | bytes 110600 | tf_op jit(solution)/shard_map/ppermute | solution.py:19
  141.7 7.7 %concatenate.24 = f32[112131]{0:T(1024)} concatenate(f32[192]{0:T(256)S(1)} %reshape.767, f32[27648]{0:T(1024)S(1)} %reshape.789, f32[288]{0:T(512)S(1)} %reduce_sum.330, f32[675]{0:T(1024)S(1)} %reshape.770, f32[9216]{0:T(1024)S(1)} %reshape.791, f32[36864]{0:T(1024)S(1)} %reshape.793, f32[384]{0:T(512)S(1)} %copy-done.84, f32[36864]{0:T(1024)S(1)} %reshape.795), dimensions={0} | concatenate | bytes 897048 | tf_op jit(solution)/shard_map/concatenate | solution.py:154
  163.5 7.8 %concatenate.23 = f32[112131]{0:T(1024)} concatenate(f32[192]{0:T(256)S(1)} %reshape.755, f32[27648]{0:T(1024)S(1)} %reshape.781, f32[288]{0:T(512)S(1)} %reduce_sum.321, f32[675]{0:T(1024)S(1)} %reshape.758, f32[9216]{0:T(1024)S(1)} %reshape.783, f32[36864]{0:T(1024)S(1)} %reshape.785, f32[384]{0:T(512)S(1)} %get-tuple-element.128, f32[36864]{0:T(1024)S(1)} %reshape.787), dimensions={0} | concatenate | bytes 897048 | tf_op jit(solution)/shard_map/concatenate | solution.py:154
  172.8 258.4 %all-reduce.18.cloned.1.call-done = (f32[112131]{0:T(1024)}, f32[112131]{0:T(1024)}) async-done(((f32[112131]{0:T(1024)}, f32[112131]{0:T(1024)}), (f32[112131]{0:T(1024)}, f32[112131]{0:T(1024)})) %all-reduce.18.cloned.1.call-update) | async-done | bytes 897064 | tf_op jit(solution)/shard_map/psum | solution.py:215
  (405 shorter events, 92.4 us)
Async XLA Ops:
  7.2 424.0 %all-reduce.18.cloned.1.call-start = ((), (), s32[]{:S(2)}) async-start(), calls=%async_computation | async-start | bytes 1802240 | tf_op jit(solution)/shard_map/psum | solution.py:215
  10.1 43.1 %copy-start.74 = (f32[96]{0:T(128)}, f32[96]{0:T(128)S(1)}, u32[]{:S(2)}) copy-start(f32[96]{0:T(128)S(1)} %get-tuple-element.113) | copy-start | bytes 1156
  12.2 33.7 %copy-start.11 = (f32[2,6,8,8]{3,1,2,0:T(8,128)}, f32[2,6,8,8]{3,1,2,0:T(8,128)S(1)}, u32[]{:S(2)}) copy-start(f32[2,6,8,8]{3,1,2,0:T(8,128)S(1)} %broadcast_multiply_fusion.2) | copy-start | bytes 9220
  13.7 23.2 %copy-start.69 = (s32[64,64]{1,0:T(8,128)}, s32[64,64]{1,0:T(8,128)S(1)}, u32[]{:S(2)}) copy-start(s32[64,64]{1,0:T(8,128)S(1)} %add_add_fusion.8) | copy-start | bytes 49156
  24.5 15.3 %collective-permute-start.1 = (bf16[4,48,96]{2,1,0:T(8,128)(2,1)S(1)}, bf16[4,48,96]{2,1,0:T(8,128)(2,1)S(1)}, u32[]{:S(2)}, u32[]{:S(2)}) collective-permute-start(bf16[4,48,96]{2,1,0:T(8,128)(2,1)S(1)} %bitcast.371), channel_id=1, source_target_pairs={{32,0},{64,32},{96,64},{128,96},{160,128},{192,160},{224,192},{33,... | collective-permute-start | bytes 110600 | tf_op jit(solution)/shard_map/ppermute | solution.py:20
  25.9 13.9 %collective-permute-start = (bf16[4,48,96]{2,1,0:T(8,128)(2,1)S(1)}, bf16[4,48,96]{2,1,0:T(8,128)(2,1)S(1)}, u32[]{:S(2)}, u32[]{:S(2)}) collective-permute-start(bf16[4,48,96]{2,1,0:T(8,128)(2,1)S(1)} %bitcast.372), channel_id=1, source_target_pairs={{0,32},{32,64},{64,96},{96,128},{128,160},{160,192},{192,224},{1,3... | collective-permute-start | bytes 110600 | tf_op jit(solution)/shard_map/ppermute | solution.py:19
  36.9 11.3 %copy-start.58 = (bf16[16,48,96]{2,1,0:T(8,128)(2,1)S(1)}, bf16[16,48,96]{2,1,0:T(8,128)(2,1)}, u32[]{:S(2)}) copy-start(bf16[16,48,96]{2,1,0:T(8,128)(2,1)} %param.11) | copy-start | bytes 442372
  39.9 11.6 %collective-permute-start.2 = (bf16[24,4,96]{2,1,0:T(4,128)(2,1)S(1)}, bf16[24,4,96]{2,1,0:T(4,128)(2,1)S(1)}, u32[]{:S(2)}, u32[]{:S(2)}) collective-permute-start(bf16[24,4,96]{2,1,0:T(4,128)(2,1)S(1)} %get-tuple-element.86), channel_id=1, source_target_pairs={{0,1},{1,2},{2,3},{3,4},{4,5},{5,6},{6,7},{7,8},{8,9},{9,10},{10,1... | collective-permute-start | bytes 55304 | tf_op jit(solution)/shard_map/ppermute | solution.py:19
  43.9 7.6 %collective-permute-start.3 = (bf16[24,4,96]{2,1,0:T(4,128)(2,1)S(1)}, bf16[24,4,96]{2,1,0:T(4,128)(2,1)S(1)}, u32[]{:S(2)}, u32[]{:S(2)}) collective-permute-start(bf16[24,4,96]{2,1,0:T(4,128)(2,1)S(1)} %get-tuple-element.87), channel_id=1, source_target_pairs={{1,0},{2,1},{3,2},{4,3},{5,4},{6,5},{7,6},{8,7},{9,8},{10,9},{11,1... | collective-permute-start | bytes 55304 | tf_op jit(solution)/shard_map/ppermute | solution.py:20
  121.1 7.0 %collective-permute-start.4 = (bf16[24,4,96]{2,1,0:T(4,128)(2,1)S(1)}, bf16[24,4,96]{2,1,0:T(4,128)(2,1)S(1)}, u32[]{:S(2)}, u32[]{:S(2)}) collective-permute-start(bf16[24,4,96]{2,1,0:T(4,128)(2,1)S(1)} %get-tuple-element.82), channel_id=1, source_target_pairs={{0,1},{1,2},{2,3},{3,4},{4,5},{5,6},{6,7},{7,8},{8,9},{9,10},{10,1... | collective-permute-start | bytes 55304 | tf_op jit(solution)/shard_map/ppermute | solution.py:19
  124.8 5.1 %collective-permute-start.5 = (bf16[24,4,96]{2,1,0:T(4,128)(2,1)S(1)}, bf16[24,4,96]{2,1,0:T(4,128)(2,1)S(1)}, u32[]{:S(2)}, u32[]{:S(2)}) collective-permute-start(bf16[24,4,96]{2,1,0:T(4,128)(2,1)S(1)} %get-tuple-element.83), channel_id=1, source_target_pairs={{1,0},{2,1},{3,2},{4,3},{5,4},{6,5},{7,6},{8,7},{9,8},{10,9},{11,1... | collective-permute-start | bytes 55304 | tf_op jit(solution)/shard_map/ppermute | solution.py:20
  128.1 11.9 %copy-start.85 = (f32[96]{0:T(128)S(1)}, f32[96]{0:T(128)}, u32[]{:S(2)}) copy-start(f32[96]{0:T(128)} %get-tuple-element.56) | copy-start | bytes 1156
  128.1 11.9 %copy-start.86 = (f32[96]{0:T(128)S(1)}, f32[96]{0:T(128)}, u32[]{:S(2)}) copy-start(f32[96]{0:T(128)} %get-tuple-element.50) | copy-start | bytes 1156
  128.2 11.9 %copy-start.65 = (f32[384,96]{0,1:T(8,128)S(1)}, f32[384,96]{0,1:T(8,128)}, u32[]{:S(2)}) copy-start(f32[384,96]{0,1:T(8,128)} %fusion.73) | copy-start | bytes 442372
  130.0 10.4 %copy-start.66 = (bf16[768,96]{0,1:T(8,128)(2,1)S(1)}, bf16[768,96]{0,1:T(8,128)(2,1)}, u32[]{:S(2)}) copy-start(bf16[768,96]{0,1:T(8,128)(2,1)} %fusion.65) | copy-start | bytes 442372
  130.0 11.2 %copy-start.44 = (f32[96,384]{1,0:T(8,128)S(1)}, f32[96,384]{1,0:T(8,128)}, u32[]{:S(2)}) copy-start(f32[96,384]{1,0:T(8,128)} %fusion.72) | copy-start | bytes 442372
  130.0 11.2 %copy-start.60 = (f32[96,96]{1,0:T(8,128)S(1)}, f32[96,96]{1,0:T(8,128)}, u32[]{:S(2)}) copy-start(f32[96,96]{1,0:T(8,128)} %fusion.77) | copy-start | bytes 110596
  130.1 11.4 %copy-start.38 = (f32[96,288]{1,0:T(8,128)S(1)}, f32[96,288]{1,0:T(8,128)}, u32[]{:S(2)}) copy-start(f32[96,288]{1,0:T(8,128)} %fusion.74) | copy-start | bytes 331780
  130.1 11.6 %copy-start.84 = (f32[384]{0:T(512)S(1)}, f32[384]{0:T(512)}, u32[]{:S(2)}) copy-start(f32[384]{0:T(512)} %get-tuple-element.126) | copy-start | bytes 4612
  130.2 19.3 %collective-permute-start.6 = (bf16[4,48,96]{2,1,0:T(8,128)(2,1)S(1)}, bf16[4,48,96]{2,1,0:T(8,128)(2,1)S(1)}, u32[]{:S(2)}, u32[]{:S(2)}) collective-permute-start(bf16[4,48,96]{2,1,0:T(8,128)(2,1)S(1)} %get-tuple-element.84), channel_id=1, source_target_pairs={{0,32},{32,64},{64,96},{96,128},{128,160},{160,192},{192,224},{1,3... | collective-permute-start | bytes 110600 | tf_op jit(solution)/shard_map/ppermute | solution.py:19
  138.8 10.7 %collective-permute-start.7 = (bf16[4,48,96]{2,1,0:T(8,128)(2,1)S(1)}, bf16[4,48,96]{2,1,0:T(8,128)(2,1)S(1)}, u32[]{:S(2)}, u32[]{:S(2)}) collective-permute-start(bf16[4,48,96]{2,1,0:T(8,128)(2,1)S(1)} %get-tuple-element.85), channel_id=1, source_target_pairs={{32,0},{64,32},{96,64},{128,96},{160,128},{192,160},{224,192},{33,... | collective-permute-start | bytes 110600 | tf_op jit(solution)/shard_map/ppermute | solution.py:20
  163.0 8.3 %copy-start.26 = (f32[768,96]{0,1:T(8,128)S(1)}, f32[768,96]{0,1:T(8,128)}, u32[]{:S(2)}) copy-start(f32[768,96]{0,1:T(8,128)} %copy.243) | copy-start | bytes 884740
  163.0 8.3 %copy-start.72 = (f32[768]{0:T(1024)S(1)}, f32[768]{0:T(1024)}, u32[]{:S(2)}) copy-start(f32[768]{0:T(1024)} %div.191) | copy-start | bytes 9220
  431.2 10.8 %copy-start.46 = (f32[112131]{0:T(1024)S(1)}, f32[112131]{0:T(1024)}, u32[]{:S(2)}) copy-start(f32[112131]{0:T(1024)} %get-tuple-element.63) | copy-start | bytes 1345576
  (75 other events, 142.4 us)
Sparse Core Ops, SparseCore 0:
  171.4 259.7 all-reduce.17
where the time goes:
time: 458 us; the launch traced here: 456 us
  waiting for transfers between devices  260 us (57%)
  local copies, waits for them, and re-layouts  84.4 us (18%)
  matrix products  37 us (8%)
  starting transfers between devices  32.9 us (7%)
  other arithmetic  25.1 us (5%)
  between operations  16 us (3%)
    psum x1, waiting for transfers between devices, body(): lax.psum((lower_flat, upper_flat), ('row', 'col'))  258 us
    ppermute x4, starting transfers between devices, padded_2(): before = lax.ppermute(last, axis, up)  26.4 us
    reshape x4, local copies, waits for them, and re-layouts, attend(): triple = triple.reshape(win_count, win_tokens, 3, head_count, head_size)  16.9 us
    concatenate x2, local copies, waits for them, and re-layouts, flatten(): jnp.concatenate([part.astype(jnp.float32).reshape(-1) for part in parts])  15.5 us
    unnamed x182, local copies, waits for them, and re-layouts  11 us
    slice x14, local copies, waits for them, and re-layouts, unflatten(): pieces.append(flat_vec[offset:offset + length].reshape(like.shape))  10.9 us
  transfers between devices with their start and end apart: 9, of which 2 were waited for; matrix products, arithmetic and copies ran while one was open for 5% of the time, Pallas kernels for 0%

commit v1 on v0

v1 whole, which is shorter than its diff:
```python
import jax
import jax.numpy as jnp
from jax import lax
from jax.experimental import pallas as pl
from jax.experimental.pallas import tpu as pltpu
from jax.sharding import Mesh
from jax.sharding import PartitionSpec as P

C = 96
HEADS = 3
HEAD = 32
HID = 384
WIN = 8
TH = 16
TW = 48
AUG = 112
PAIR = 128
ROWS = 1024
PEERS = 128
GROUP = 256
LOG2E = 1.4426950408889634
SCALE = HEAD**-0.5
FAR = -1e30
F32 = jnp.float32
BF16 = jnp.bfloat16

LOWER = [(i, j) for i in (1, 2) for j in range(1, 7)]
LOWER += [(i, j) for i in range(4) for j in range(8) if (i, j) not in LOWER]
UPPER = [(i, j) for i in (0, 1) for j in range(6)]
UPPER += [(2, j) for j in range(7)] + [(0, 6), (1, 6)]
LOWER_GROUPS = 8
OWN_GROUPS = 3
UPPER_GROUPS = 6


def dot(a, b):
    return jnp.dot(a, b, preferred_element_type=F32)


def dot_nt(a, b):
    return lax.dot_general(a, b, (((1,), (1,)), ((), ())), preferred_element_type=F32)


def split3(v):
    hi = v.astype(BF16)
    rest = v - hi.astype(F32)
    mid = rest.astype(BF16)
    return hi, mid, (rest - mid.astype(F32)).astype(BF16)


def transposed(v):
    return jnp.transpose(v.astype(F32)).astype(BF16)


def augmented(weight, bias):
    hi, mid, lo = split3(bias)
    rows = lax.broadcasted_iota(jnp.int32, (AUG - C, bias.shape[1]), 0)
    extra = jnp.where(
        rows == 0,
        hi.astype(F32),
        jnp.where(rows == 1, mid.astype(F32), jnp.where(rows == 2, lo.astype(F32), 0.0)),
    )
    return transposed(jnp.concatenate([weight.astype(F32), extra], 0))


def lane_code(lanes):
    token = lanes % 64
    return (token // WIN) * 15 + token % WIN


def expand_table(row):
    parts = []
    for kr in range(WIN):
        wide = jnp.broadcast_to(row, (WIN, 256))
        parts.append(pltpu.roll(wide, (15 * kr - 112) % 256, 1, stride=1, stride_axis=0))
    rolled = jnp.concatenate(parts, 0)
    lane = lax.broadcasted_iota(jnp.int32, (256, PAIR), 0)
    query = lax.broadcasted_iota(jnp.int32, (256, PAIR), 1)
    onehot = (lane == lane_code(query)).astype(BF16)
    hi, mid, lo = split3(rolled)
    both = dot(hi, onehot) + dot(mid, onehot) + dot(lo, onehot)
    first = lax.broadcasted_iota(jnp.int32, both.shape, 1) < 64
    return jnp.concatenate([jnp.where(first, both, FAR), jnp.where(first, FAR, both)], 0) * LOG2E


def fold_table(acc):
    both = acc[:64] + acc[64:]
    lane = lax.broadcasted_iota(jnp.int32, (PAIR, 256), 1)
    query = lax.broadcasted_iota(jnp.int32, (PAIR, 256), 0)
    onehot = (lane == 112 - lane_code(query)).astype(BF16)
    hi, mid, _ = split3(both)
    wide = dot(hi, onehot) + dot(mid, onehot)
    total = jnp.zeros((WIN, 256), F32)
    for kr in range(WIN):
        total += pltpu.roll(
            wide[kr * WIN : (kr + 1) * WIN], 15 * kr, 1, stride=1, stride_axis=0
        )
    return jnp.sum(total, 0, keepdims=True)


def reverse_lanes(rows):
    a = lax.broadcasted_iota(jnp.int32, (256, 256), 0)
    b = lax.broadcasted_iota(jnp.int32, (256, 256), 1)
    onehot = (a + b == 224).astype(BF16)
    hi, mid, _ = split3(rows)
    return dot(hi, onehot) + dot(mid, onehot)


def norm(x):
    mean = jnp.sum(x, 0, keepdims=True) * (1.0 / C)
    centred = x - mean
    var = jnp.sum(centred * centred, 0, keepdims=True) * (1.0 / C)
    r = lax.rsqrt(var + 1e-05)
    return centred * r, r


def norm_back(dxhat, xhat, r):
    m1 = jnp.sum(dxhat, 0, keepdims=True) * (1.0 / C)
    m2 = jnp.sum(dxhat * xhat, 0, keepdims=True) * (1.0 / C)
    return r * (dxhat - m1 - xhat * m2)


def wide_gain(gain):
    return jnp.concatenate([gain] * (GROUP // PAIR), 1)


def with_ones(v):
    return jnp.concatenate([v, jnp.ones((AUG - C, v.shape[1]), BF16)], 0)


def head_blocks(v):
    zero = jnp.zeros((HEAD, PAIR), v.dtype)
    cols = []
    for h in range(HEADS):
        rows = [v[g * HEAD : (g + 1) * HEAD] if g == h else zero for g in range(HEADS)]
        cols.append(jnp.concatenate(rows, 0))
    return jnp.concatenate(cols, 1)


def head_diagonal(v):
    return jnp.concatenate(
        [v[h * HEAD : (h + 1) * HEAD, h * PAIR : (h + 1) * PAIR] for h in range(HEADS)], 0
    )


def gelu_parts(u):
    k = 0.7978845608028654
    uu = u * u
    t = jnp.tanh(u * (k + (k * 0.044715) * uu))
    half = 0.5 + 0.5 * t
    slope = half + (half * (1.0 - t)) * u * (k + (3 * k * 0.044715) * uu)
    return u * half, slope


def forward(x, b, w, penalty):
    xhat1, r1 = norm(x)
    a = with_ones((xhat1 * wide_gain(w.gain[b, 0])).astype(BF16))
    qkv = dot(w.qkv_t[b], a).astype(BF16)
    probs, mixed, tokens = [], [], []
    for p in range(2):
        lanes = slice(p * PAIR, (p + 1) * PAIR)
        key_tok = transposed(qkv[C : 2 * C, lanes])
        scores = dot(key_tok, head_blocks(qkv[:C, lanes])) * (SCALE * LOG2E) + w.bias[b]
        if penalty is not None:
            scores = scores + jnp.concatenate([penalty[p]] * HEADS, 1)
        e = jnp.exp2(scores - jnp.max(scores, 0, keepdims=True))
        prob = (e * (1.0 / jnp.sum(e, 0, keepdims=True))).astype(BF16)
        mixed.append(head_diagonal(dot(qkv[2 * C :, lanes], prob)))
        probs.append(prob)
    mix = jnp.concatenate(mixed, 1).astype(BF16)
    h = x + dot(w.proj_t[b], mix)
    xhat2, r2 = norm(h)
    f = with_ones((xhat2 * wide_gain(w.gain[b, 1])).astype(BF16))
    u = dot(w.up_t[b], f)
    m, slope = gelu_parts(u)
    m = m.astype(BF16)
    out = h + dot(w.down_t[b], m)
    return out, (xhat1, r1, a, qkv, probs, mix, xhat2, r2, f, m, slope)


def backward(g, b, w, saved, mask):
    xhat1, r1, a, qkv, probs, mix, xhat2, r2, f, m, slope = saved

    def own(v):
        return v if mask is None else v * mask.astype(v.dtype)

    def own_pair(v, p):
        if mask is None:
            return v
        return v * jnp.concatenate([mask[:, p * PAIR : (p + 1) * PAIR]] * HEADS, 1)

    def lanes_sum(v):
        return v[:, :PAIR] + v[:, PAIR:]

    g16 = g.astype(BF16)
    du = (dot(w.down[b], g16) * slope).astype(BF16)
    w.d_down[b] += dot_nt(own(g16), m)
    w.d_up[b] += dot_nt(own(f), du)
    df = dot(w.up[b], du)
    w.d_gain[b, 1] += lanes_sum(own(df * xhat2))
    dh = g + norm_back(df * wide_gain(w.gain[b, 1]), xhat2, r2)
    dh16 = dh.astype(BF16)
    w.d_proj[b] += dot_nt(mix, own(dh16))
    dmix = dot(w.proj[b], dh16).astype(BF16)
    dq, dk, dv = [], [], []
    for p in range(2):
        lanes = slice(p * PAIR, (p + 1) * PAIR)
        val_tok = transposed(qkv[2 * C :, lanes])
        blocks = head_blocks(dmix[:, lanes])
        dprob = dot(val_tok, blocks)
        prob = probs[p].astype(F32)
        weighted = prob * dprob
        ds = weighted - prob * jnp.sum(weighted, 0, keepdims=True)
        w.d_bias[b] += own_pair(ds, p)
        ds16 = ds.astype(BF16)
        dv.append(dot_nt(blocks, probs[p]))
        dk.append(dot_nt(head_blocks(qkv[:C, lanes]), ds16) * SCALE)
        dq.append(head_diagonal(dot(qkv[C : 2 * C, lanes], ds16)) * SCALE)
    dqkv = jnp.concatenate([jnp.concatenate(v, 1) for v in (dq, dk, dv)], 0).astype(BF16)
    w.d_qkv[b] += dot_nt(own(a), dqkv)
    da = dot(w.qkv[b], dqkv)
    w.d_gain[b, 0] += lanes_sum(own(da * xhat1))
    return dh + norm_back(da * wide_gain(w.gain[b, 0]), xhat1, r1)


class Layers:
    pass


def windows_t(ref, places, r0, c0):
    tokens = []
    for i, j in places:
        block = ref[r0 + WIN * i : r0 + WIN * (i + 1), c0 + WIN * j : c0 + WIN * (j + 1), :]
        tokens.append(block.astype(F32).reshape(WIN * WIN, C))
    if len(tokens) == 1:
        tokens.append(jnp.zeros((WIN * WIN, C), F32))
    return jnp.transpose(jnp.concatenate(tokens, 0))


def windows_back(value, ref, places):
    tokens = jnp.transpose(value)
    for n, (i, j) in enumerate(places):
        block = tokens[n * 64 : (n + 1) * 64].reshape(WIN, WIN, C)
        ref[WIN * i : WIN * (i + 1), WIN * j : WIN * (j + 1), :] = block.astype(ref.dtype)


def kernel(
    place,
    region,
    cot,
    row_a,
    row_b,
    col_a,
    col_b,
    norm_gains,
    qkv_weight,
    qkv_bias,
    bias_table,
    proj_weight,
    up_weight,
    up_bias,
    down_t,
    out,
    grad_region,
    packed,
    wide_region,
    wide_cot,
    x_low,
    y_low,
    x_up,
    g_up,
    y_up,
    dx_up,
    low_field,
    out_field,
    grad_field,
    table,
    misc,
    gain,
    qkv_t,
    proj_t,
    up_t,
    down,
    bias,
    d_gain,
    d_qkv,
    d_proj,
    d_up,
    d_down,
    d_bias,
    *saves,
):
    w = Layers()
    w.qkv, w.proj, w.up, w.down_t = qkv_weight, proj_weight, up_weight, down_t
    w.gain, w.qkv_t, w.proj_t, w.up_t, w.down, w.bias = gain, qkv_t, proj_t, up_t, down, bias
    w.d_gain, w.d_qkv, w.d_proj = d_gain, d_qkv, d_proj
    w.d_up, w.d_down, w.d_bias = d_up, d_down, d_bias
    s_prob = saves[4]
    first_row, last_row = place[0] == 0, place[0] == place[2] - 1
    first_col, last_col = place[1] == 0, place[1] == place[3] - 1

    above, below = sides(place[0], row_a[...], row_b[...])
    left, right = sides(place[1], col_a[...], col_b[...])
    inner = slice(8, 8 + TW)
    wide_region[0:8, inner, :] = above[0:8].astype(F32)
    wide_region[8:24, inner, :] = region[...].astype(F32)
    wide_region[24:32, inner, :] = below[0:8].astype(F32)
    wide_region[:, 0:8, :] = left[0:32].astype(F32)
    wide_region[:, 8 + TW :, :] = right[0:32].astype(F32)
    wide_cot[0:4, inner, :] = above[8:12].astype(F32)
    wide_cot[4:20, inner, :] = cot[...].astype(F32)
    wide_cot[20:24, inner, :] = below[8:12].astype(F32)
    wide_cot[:, 0:8, :] = left[32:56].astype(F32)
    wide_cot[:, 8 + TW :, :] = right[32:56].astype(F32)

    for ref in (d_gain, d_qkv, d_proj, d_up, d_down, d_bias, table, misc):
        ref[...] = jnp.zeros(ref.shape, F32)
    for b in range(2):
        qkv_t[b] = augmented(qkv_weight[b], qkv_bias[b : b + 1, :])
        up_t[b] = augmented(up_weight[b], up_bias[b : b + 1, :])
        proj_t[b] = transposed(proj_weight[b])
        down[b] = transposed(down_t[b])
        for n in range(2):
            row = jnp.broadcast_to(norm_gains[b, n : n + 1, :], (PAIR, C))
            gain[b, n] = jnp.transpose(row)
        for h in range(HEADS):
            table[b, h : h + 1, 0 : bias_table.shape[2]] = bias_table[h, b : b + 1, :]
            bias[b, :, h * PAIR : (h + 1) * PAIR] = expand_table(table[b, h : h + 1, :])

    for n in range(2 * LOWER_GROUPS):
        value = windows_t(wide_region, LOWER[2 * n : 2 * n + 2], 0, 0)
        x_low[n // 2, :, (n % 2) * PAIR : (n % 2 + 1) * PAIR] = value

    def own_step(g, _):
        y, saved = forward(x_low[g], 0, w, None)
        y_low[g] = y.astype(BF16).astype(F32)
        for ref, value in zip(saves, saved):
            if ref is s_prob:
                for p in range(2):
                    ref[g, p] = value[p]
            else:
                ref[g] = value
        return 0

    lax.fori_loop(0, OWN_GROUPS, own_step, 0)

    def halo_step(g, _):
        y, _ = forward(x_low[g], 0, w, None)
        y_low[g] = y.astype(BF16).astype(F32)
        return 0

    lax.fori_loop(OWN_GROUPS, LOWER_GROUPS, halo_step, 0)

    for n in range(2 * LOWER_GROUPS):
        value = y_low[n // 2, :, (n % 2) * PAIR : (n % 2 + 1) * PAIR]
        windows_back(value, low_field, LOWER[2 * n : 2 * n + 2])

    for n in range(2 * UPPER_GROUPS):
        lanes = slice((n % 2) * PAIR, (n % 2 + 1) * PAIR)
        places = UPPER[2 * n : 2 * n + 2]
        if places:
            x_up[n // 2, :, lanes] = windows_t(low_field, places, 4, 4)
            g_up[n // 2, :, lanes] = windows_t(wide_cot, places, 0, 4)
        else:
            x_up[n // 2, :, lanes] = jnp.zeros((C, PAIR), F32)
            g_up[n // 2, :, lanes] = jnp.zeros((C, PAIR), F32)

    def edges(s):
        top = first_row & ((s < 6) | (s == 19))
        bottom = last_row & (s >= 12) & (s < 19)
        left = first_col & ((s == 0) | (s == 6) | (s == 12))
        right = last_col & (s >= 18) & (s < 21)
        return [jnp.where(v, FAR, 0.0) for v in (top, bottom, left, right)]

    def upper_step(g, _):
        key = lax.broadcasted_iota(jnp.int32, (PAIR, PAIR), 0)
        upper_half = ((key // WIN) % WIN) < 4
        left_half = (key % WIN) < 4
        penalty = []
        for p in range(2):
            one, two = edges(4 * g + 2 * p), edges(4 * g + 2 * p + 1)
            top, bottom, left, right = [jnp.where(key < 64, v, u) for v, u in zip(one, two)]
            penalty.append(
                jnp.where(upper_half, top, bottom) + jnp.where(left_half, left, right)
            )
        slot = 4 * g + lax.broadcasted_iota(jnp.int32, (1, GROUP), 1) // 64
        row_own = jnp.where(last_row, 1.0, 0.0)
        col_own = jnp.where(last_col, 1.0, 0.0)
        mask = jnp.where(
            slot < 12,
            1.0,
            jnp.where(
                slot < 18,
                row_own,
                jnp.where(slot < 19, row_own * col_own, jnp.where(slot < 21, col_own, 0.0)),
            ),
        )
        y, saved = forward(x_up[g], 1, w, penalty)
        y_up[g] = y
        dx_up[g] = backward(g_up[g], 1, w, saved, mask)
        return 0

    lax.fori_loop(0, UPPER_GROUPS, upper_step, 0)

    for n in range(2 * UPPER_GROUPS):
        lanes = slice((n % 2) * PAIR, (n % 2 + 1) * PAIR)
        places = UPPER[2 * n : 2 * n + 2]
        if places:
            windows_back(y_up[n // 2, :, lanes], out_field, places)
            windows_back(dx_up[n // 2, :, lanes], grad_field, places)
    out[...] = out_field[4 : 4 + TH, 4 : 4 + TW, :].astype(BF16)

    for n in range(2 * OWN_GROUPS):
        lanes = slice((n % 2) * PAIR, (n % 2 + 1) * PAIR)
        g_up[n // 2, :, lanes] = windows_t(grad_field, UPPER[2 * n : 2 * n + 2], 4, 4)

    def lower_step(g, _):
        saved = [[ref[g, 0], ref[g, 1]] if ref is s_prob else ref[g] for ref in saves]
        dx_up[g] = backward(g_up[g], 0, w, saved, None)
        return 0

    lax.fori_loop(0, OWN_GROUPS, lower_step, 0)

    for n in range(2 * OWN_GROUPS):
        lanes = slice((n % 2) * PAIR, (n % 2 + 1) * PAIR)
        windows_back(dx_up[n // 2, :, lanes], grad_region, UPPER[2 * n : 2 * n + 2])

    for b in range(2):
        for j in range(3):
            lanes = slice(j * PAIR, (j + 1) * PAIR)
            packed[b, j * C : (j + 1) * C, :] = d_up[b, 0:C, lanes].astype(BF16)
            packed[b, 288 + j * C : 288 + (j + 1) * C, :] = d_down[b, :, lanes].astype(BF16)
            misc[b, 3 + j : 4 + j, :] = d_up[b, C : C + 1, lanes]
        for j in range(2):
            lanes = slice(j * PAIR, (j + 1) * PAIR)
            packed[b, 576 + j * C : 576 + (j + 1) * C, :] = d_qkv[b, 0:C, lanes].astype(BF16)
            misc[b, j : j + 1, :] = d_qkv[b, C : C + 1, lanes]
        last = jnp.concatenate([d_qkv[b, 0:C, 256:288], d_proj[b]], 1)
        packed[b, 768:864, :] = last.astype(BF16)
        misc[b, 2:3, 0:32] = d_qkv[b, C : C + 1, 256:288]
        for n in range(2):
            column = jnp.sum(jnp.transpose(d_gain[b, n]), 0, keepdims=True)
            misc[b, 6 + n : 7 + n, 0:C] = column
        for h in range(HEADS):
            table[b, h : h + 1, :] = fold_table(d_bias[b, :, h * PAIR : (h + 1) * PAIR])
        rows = reverse_lanes(table[b])
        misc[b, 8:16, :] = rows[:, 0:PAIR]
        misc[b, 16:24, :] = rows[:, PAIR:]
        packed[b, 864:896, :] = misc[b].astype(BF16)
        packed[b, 896:ROWS, :] = jnp.zeros((ROWS - 896, PAIR), BF16)


VMEM = pl.BlockSpec(memory_space=pltpu.VMEM)
SMEM = pl.BlockSpec(memory_space=pltpu.SMEM)


def local(place, arrays):
    shapes = [
        ((TH + 16, TW + 16, C), F32),
        ((TH + 8, TW + 16, C), F32),
        ((LOWER_GROUPS, C, GROUP), F32),
        ((LOWER_GROUPS, C, GROUP), F32),
        ((UPPER_GROUPS, C, GROUP), F32),
        ((UPPER_GROUPS, C, GROUP), F32),
        ((UPPER_GROUPS, C, GROUP), F32),
        ((UPPER_GROUPS, C, GROUP), F32),
        ((TH + 16, TW + 16, C), F32),
        ((TH + 8, TW + 8, C), F32),
        ((TH + 8, TW + 8, C), F32),
        ((2, 8, 256), F32),
        ((2, 32, PAIR), F32),
        ((2, 2, C, PAIR), F32),
        ((2, 3 * C, AUG), BF16),
        ((2, C, C), BF16),
        ((2, HID, AUG), BF16),
        ((2, HID, C), BF16),
        ((2, PAIR, HEADS * PAIR), F32),
        ((2, 2, C, PAIR), F32),
        ((2, AUG, 3 * C), F32),
        ((2, C, C), F32),
        ((2, AUG, HID), F32),
        ((2, C, HID), F32),
        ((2, PAIR, HEADS * PAIR), F32),
        ((OWN_GROUPS, C, GROUP), F32),
        ((OWN_GROUPS, 1, GROUP), F32),
        ((OWN_GROUPS, AUG, GROUP), BF16),
        ((OWN_GROUPS, 3 * C, GROUP), BF16),
        ((OWN_GROUPS, 2, PAIR, HEADS * PAIR), BF16),
        ((OWN_GROUPS, C, GROUP), BF16),
        ((OWN_GROUPS, C, GROUP), F32),
        ((OWN_GROUPS, 1, GROUP), F32),
        ((OWN_GROUPS, AUG, GROUP), BF16),
        ((OWN_GROUPS, HID, GROUP), BF16),
        ((OWN_GROUPS, HID, GROUP), F32),
    ]
    return pl.pallas_call(
        kernel,
        out_shape=(
            jax.ShapeDtypeStruct((TH, TW, C), BF16),
            jax.ShapeDtypeStruct((TH, TW, C), F32),
            jax.ShapeDtypeStruct((2, ROWS, PAIR), BF16),
        ),
        in_specs=[SMEM] + [VMEM] * len(arrays),
        out_specs=[VMEM] * 3,
        scratch_shapes=[pltpu.VMEM(shape, kind) for shape, kind in shapes],
        compiler_params=pltpu.CompilerParams(vmem_limit_bytes=48 * 1024 * 1024),
        name="blocks",
    )(place, *arrays)


def sides(position, from_a, from_b):
    even = position % 2 == 0
    return jnp.where(even, from_b, from_a), jnp.where(even, from_a, from_b)


def row_kernel(place, region, cot, send_a, send_b):
    even = place[0] % 2 == 0
    for dst, top in ((send_a, jnp.logical_not(even)), (send_b, even)):
        dst[0:8] = jnp.where(top, region[0:8], region[8:16])
        dst[8:12] = jnp.where(top, cot[0:4], cot[12:16])


def col_kernel(place, region, cot, row_a, row_b, send_a, send_b):
    above, below = sides(place[0], row_a[...], row_b[...])
    even = place[1] % 2 == 0
    for dst, left in ((send_a, jnp.logical_not(even)), (send_b, even)):
        for rows, value in (
            (slice(0, 8), above[0:8]),
            (slice(8, 24), region[...]),
            (slice(24, 32), below[0:8]),
            (slice(32, 36), above[8:12]),
            (slice(36, 52), cot[...]),
            (slice(52, 56), below[8:12]),
        ):
            dst[rows] = jnp.where(left, value[:, 0:8], value[:, TW - 8 :])


def unpack_kernel(
    place, mine, other, gains, qkv, qkv_bias, table, proj, up, up_bias, down_t
):
    core = place[1] % 2
    for b in range(2):
        flat = jnp.where(core == b, mine[...], other[...]).astype(F32)
        misc = flat[864:896]
        for j in range(3):
            lanes = slice(j * PAIR, (j + 1) * PAIR)
            up[b, :, lanes] = flat[j * C : (j + 1) * C]
            down_t[b, :, lanes] = flat[288 + j * C : 288 + (j + 1) * C]
            up_bias[b : b + 1, lanes] = misc[3 + j : 4 + j]
        for j in range(2):
            lanes = slice(j * PAIR, (j + 1) * PAIR)
            qkv[b, :, lanes] = flat[576 + j * C : 576 + (j + 1) * C]
            qkv_bias[b : b + 1, lanes] = misc[j : j + 1]
        last = flat[768:864]
        qkv[b, :, 256:288] = last[:, 0:32]
        proj[b] = last[:, 32:PAIR]
        qkv_bias[b : b + 1, 256:288] = misc[2:3, 0:32]
        for n in range(2):
            gains[b, n : n + 1, :] = misc[6 + n : 7 + n, 0:C]
        for h in range(HEADS):
            table[h, b : b + 1, 0:PAIR] = misc[8 + h : 9 + h]
            table[h, b : b + 1, PAIR:225] = misc[16 + h : 17 + h, 0:97]


def near(count):
    return [(i, i ^ 1) for i in range(count)]


def far(count):
    return [(i, ((i - 1) ^ 1) + 1) for i in range(1, count - 1)]


def swap(pair, axes, count):
    return lax.ppermute(pair[0], axes, near(count)), lax.ppermute(pair[1], axes, far(count))


def body(region, cotangent, gains, qkv, qkv_bias, table, proj, up, up_bias, down):
    col_axes = ("col_half", "core")
    rows, cols = lax.axis_size("row"), lax.axis_size(col_axes)
    core = lax.axis_index("core")
    place = jnp.stack(
        [lax.axis_index("row"), lax.axis_index(col_axes), jnp.int32(rows), jnp.int32(cols)]
    ).astype(jnp.int32)
    strip = jax.ShapeDtypeStruct((12, TW, C), BF16)
    send = pl.pallas_call(
        row_kernel,
        out_shape=(strip, strip),
        in_specs=[SMEM, VMEM, VMEM],
        out_specs=[VMEM] * 2,
        name="row_strips",
    )(place, region, cotangent)
    row_got = swap(send, "row", rows)
    strip = jax.ShapeDtypeStruct((56, 8, C), BF16)
    send = pl.pallas_call(
        col_kernel,
        out_shape=(strip, strip),
        in_specs=[SMEM] + [VMEM] * 4,
        out_specs=[VMEM] * 2,
        name="col_strips",
    )(place, region, cotangent, *row_got)
    col_got = swap(send, col_axes, cols)
    table_t = jnp.transpose(table, (1, 0, 2))
    down_t = jnp.transpose(down, (0, 2, 1))
    out, grad_region, packed = local(
        place,
        (region, cotangent, *row_got, *col_got)
        + (gains, qkv, qkv_bias, table_t, proj, up, up_bias, down_t),
    )
    keep = lax.dynamic_index_in_dim(packed, core, 0, keepdims=False)
    give = lax.dynamic_index_in_dim(packed, 1 - core, 0, keepdims=False)
    got = lax.ppermute(give, "core", near(2))
    share = (keep.astype(F32) + got.astype(F32)).astype(BF16).reshape(PEERS, -1, PAIR)
    peers = ("row", "col_half")
    parts = lax.all_to_all(share, peers, 0, 0)
    part = jnp.sum(parts.astype(F32), 0, keepdims=True).astype(BF16)
    mine = lax.all_to_all(jnp.broadcast_to(part, share.shape), peers, 0, 0)
    mine = mine.reshape(ROWS, PAIR)
    other = lax.ppermute(mine, "core", near(2))
    grads = pl.pallas_call(
        unpack_kernel,
        out_shape=tuple(
            jax.ShapeDtypeStruct(shape, F32)
            for shape in (
                (2, 2, C),
                (2, C, 3 * C),
                (2, 3 * C),
                (HEADS, 2, 225),
                (2, C, C),
                (2, C, HID),
                (2, HID),
                (2, C, HID),
            )
        ),
        in_specs=[SMEM, VMEM, VMEM],
        out_specs=[VMEM] * 8,
        name="unpack",
    )(place, mine, other)
    d_gains, d_qkv, d_qkv_bias, d_table, d_proj, d_up, d_up_bias, d_down_t = grads
    return (
        out,
        grad_region,
        d_gains,
        d_qkv,
        d_qkv_bias,
        jnp.transpose(d_table, (1, 0, 2)),
        d_proj,
        d_up,
        d_up_bias,
        jnp.transpose(d_down_t, (0, 2, 1)),
    )


def solution(mesh):
    rows, cols = mesh.devices.shape
    fine = Mesh(mesh.devices.reshape(rows, cols // 2, 2), ("row", "col_half", "core"))
    tile = P("row", ("col_half", "core"), None)
    return jax.shard_map(
        body,
        mesh=fine,
        in_specs=(tile, tile) + (P(),) * 8,
        out_specs=(tile, tile) + (P(),) * 8,
        check_vma=False,
    )
```

time: 458 us -> 132 us (0.29)
  waiting for transfers between devices: 260 us -> 8.38 us
  local copies, waits for them, and re-layouts: 84.4 us -> 4.52 us
  blocking collectives: 0 us -> 56.4 us
  Pallas kernels: 0 us -> 43.3 us
  matrix products: 37 us -> 0 us
  other arithmetic: 25.1 us -> 0.86 us
  starting transfers between devices: 32.9 us -> 17.2 us
  between operations: 16 us -> 0.78 us
    psum x1 -> x0, waiting for transfers between devices: 258 us -> none  [body(): lax.psum((lower_flat, upper_flat), ('row', 'col'))]
    all_to_all x0 -> x2, blocking collectives: none -> 56.4 us  [the longest x1 37.8 us: body(): parts = lax.all_to_all(share, peers, 0, 0)]
    pallas_call x0 -> x4, Pallas kernels: none -> 43.3 us  [the longest x1 37.5 us: local(): pl.pallas_call(kernel, out_shape=(jax.ShapeDtypeStruct((TH, TW, C), BF16)...]
    dot_general x38 -> x0, matrix products: 34 us -> none  [the longest x4 8.48 us: position_bias(): return jnp.einsum('qkt,ht->hqk', onehot, table, precision=HIGHEST)]
    reshape x30 -> x0, local copies, waits for them, and re-layouts: 26.9 us -> none  [the longest x4 16.9 us: attend(): triple = triple.reshape(win_count, win_tokens, 3, head_count, head_size)]
    ppermute x8 -> x6, starting transfers between devices: 32.9 us -> 17.2 us  [the longest x2 9.61 us: swap(): lax.ppermute(pair[0], axes, near(count))]
    concatenate x2 -> x0, local copies, waits for them, and re-layouts: 15.5 us -> none  [flatten(): jnp.concatenate([part.astype(jnp.float32).reshape(-1) for part in parts])]
    slice x24 -> x0, local copies, waits for them, and re-layouts: 15.5 us -> none  [the longest x14 10.9 us: unflatten(): pieces.append(flat_vec[offset:offset + length].reshape(like.shape))]
  transfers between devices with their start and end apart: 9 -> 6, of which waited for: 2 -> 4; matrix products, arithmetic and copies ran while one was open for 5% -> 0% of each run, Pallas kernels for 0% -> 0%
where the time goes in v1:
time: 132 us; the launch traced here: 131 us
  blocking collectives  56.4 us (43%)
  Pallas kernels  43.3 us (33%)
  starting transfers between devices  17.2 us (13%)
  waiting for transfers between devices  8.38 us (6%)
  local copies, waits for them, and re-layouts  4.52 us (3%)
    all_to_all x1, blocking collectives, body(): parts = lax.all_to_all(share, peers, 0, 0)  37.8 us
    pallas_call x1, Pallas kernels, local(): pl.pallas_call(kernel, out_shape=(jax.ShapeDtypeStruct((TH, TW, C), BF16)...  37.5 us
    all_to_all x1, blocking collectives, body(): mine = lax.all_to_all(jnp.broadcast_to(part, share.shape), peers, 0, 0)  18.5 us
    ppermute x2, starting transfers between devices, swap(): lax.ppermute(pair[0], axes, near(count))  9.61 us
    unnamed x34, local copies, waits for them, and re-layouts  4.47 us
    ppermute x2, starting transfers between devices, swap(): lax.ppermute(pair[1], axes, far(count))  3.94 us
    ppermute x1, starting transfers between devices, body(): other = lax.ppermute(mine, 'core', near(2))  3.56 us
    ppermute x2, waiting for transfers between devices, swap(): lax.ppermute(pair[1], axes, far(count))  3.28 us
  transfers between devices with their start and end apart: 6, of which 4 were waited for; matrix products, arithmetic and copies ran while one was open for 0% of the time, Pallas kernels for 0%

profile of v1, /device:TPU:1, one launch (start us, length us, event | category | flops | bytes accessed | tf_op | source)
XLA Modules:
  0.0 131.5 jit_solution(16975447399966818690)
XLA Ops:
  0.7 0.7 pad_add_fusion.place
  1.3 1.8 %row_strips.1 = (bf16[12,48,96]{2,1,0:T(8,128)(2,1)}, bf16[12,48,96]{2,1,0:T(8,128)(2,1)}) custom-call(s32[4]{0:T(128)} %pad_add_fusion.place, bf16[16,48,96]{2,1,0:T(8,128)(2,1)} %region.5, bf16[16,48,96]{2,1,0:T(8,128)(2,1)} %cot.5), custom_call_target="tpu_custom_call" | custom-call | tf_op jit(solution)/shard_map/row_strips/pallas_call | solution.py:585
  3.1 7.7 %collective-permute-start = (bf16[12,48,96]{2,1,0:T(8,128)(2,1)}, bf16[12,48,96]{2,1,0:T(8,128)(2,1)S(1)}, u32[]{:S(2)}, u32[]{:S(2)}) collective-permute-start(bf16[12,48,96]{2,1,0:T(8,128)(2,1)} %get-tuple-element.25), channel_id=1, source_target_pairs={{0,32},{32,0},{64,96},{96,64},{128,160},{160,128},{192,224},{224,1... | collective-permute-start | bytes 331784 | tf_op jit(solution)/shard_map/ppermute | solution.py:574
  10.9 0.8 collective-permute-start.1
  11.7 2.4 %collective-permute-done.row_a = bf16[12,48,96]{2,1,0:T(8,128)(2,1)S(1)} collective-permute-done((bf16[12,48,96]{2,1,0:T(8,128)(2,1)}, bf16[12,48,96]{2,1,0:T(8,128)(2,1)S(1)}, u32[]{:S(2)}, u32[]{:S(2)}) %collective-permute-start) | collective-permute-done | bytes 110624 | tf_op jit(solution)/shard_map/ppermute | solution.py:574
  14.1 0.7 copy-done.2
  14.8 0.7 copy-done.4
  15.4 1.9 %col_strips.1 = (bf16[56,8,96]{2,1,0:T(8,128)(2,1)}, bf16[56,8,96]{2,1,0:T(8,128)(2,1)}) custom-call(s32[4]{0:T(128)} %pad_add_fusion.place, bf16[16,48,96]{2,1,0:T(8,128)(2,1)} %region.5, bf16[16,48,96]{2,1,0:T(8,128)(2,1)} %cot.5, bf16[12,48,96]{2,1,0:T(8,128)(2,1)} %copy-done.2, bf16[12,48,96]{2,1,0:T(8,128)(2,1)} %copy-done.4), custom_call_target="tpu_custom_call" | custom-call | tf_op jit(solution)/shard_map/col_strips/pallas_call | solution.py:594
  17.4 1.9 %collective-permute-start.2 = (bf16[56,8,96]{2,1,0:T(8,128)(2,1)}, bf16[56,8,96]{2,1,0:T(8,128)(2,1)S(1)}, u32[]{:S(2)}, u32[]{:S(2)}) collective-permute-start(bf16[56,8,96]{2,1,0:T(8,128)(2,1)} %get-tuple-element.27), channel_id=1, source_target_pairs={{0,1},{1,0},{2,3},{3,2},{4,5},{5,4},{6,7},{7,6},{8,9},{9,8},{10,11... | collective-permute-start | bytes 258056 | tf_op jit(solution)/shard_map/ppermute | solution.py:574
  19.3 3.1 %collective-permute-start.3 = (bf16[56,8,96]{2,1,0:T(8,128)(2,1)}, bf16[56,8,96]{2,1,0:T(8,128)(2,1)S(1)}, u32[]{:S(2)}, u32[]{:S(2)}) collective-permute-start(bf16[56,8,96]{2,1,0:T(8,128)(2,1)} %get-tuple-element.28), channel_id=1, source_target_pairs={{1,2},{2,1},{3,4},{4,3},{5,6},{6,5},{7,8},{8,7},{9,10},{10,9},{11,... | collective-permute-start | bytes 258056 | tf_op jit(solution)/shard_map/ppermute | solution.py:574
  22.4 3.3 %collective-permute-done.3.col_b = bf16[56,8,96]{2,1,0:T(8,128)(2,1)S(1)} collective-permute-done((bf16[56,8,96]{2,1,0:T(8,128)(2,1)}, bf16[56,8,96]{2,1,0:T(8,128)(2,1)S(1)}, u32[]{:S(2)}, u32[]{:S(2)}) %collective-permute-start.3) | collective-permute-done | bytes 86048 | tf_op jit(solution)/shard_map/ppermute | solution.py:574
  25.8 0.6 copy-done.10
  26.4 0.9 copy-done.3
  27.3 0.9 copy-done.5
  28.2 37.5 %blocks.1 = (bf16[16,48,96]{2,1,0:T(8,128)(2,1)}, f32[16,48,96]{2,1,0:T(8,128)}, bf16[2,1024,128]{2,1,0:T(8,128)(2,1)S(1)}) custom-call(s32[4]{0:T(128)S(1)} %copy-done.10, bf16[16,48,96]{2,1,0:T(8,128)(2,1)S(1)} %copy-done, bf16[16,48,96]{2,1,0:T(8,128)(2,1)S(1)} %copy-done.1, bf16[12,48,96]{2,1,0:T(8,128)(2,1)S(1)} %copy-done.3, ...), custom_call_target="tpu_custom_call" | custom-call | tf_op jit(solution)/shard_map/blocks/pallas_call | solution.py:496
  65.7 0.1 collective-permute-start.4
  65.8 1.5 %collective-permute-done.4 = bf16[1024,128]{1,0:T(8,128)(2,1)S(1)} collective-permute-done((bf16[1024,128]{1,0:T(8,128)(2,1)S(1)}, bf16[1024,128]{1,0:T(8,128)(2,1)S(1)}, u32[]{:S(2)}, u32[]{:S(2)}) %collective-permute-start.4) | collective-permute-done | bytes 262176 | tf_op jit(solution)/shard_map/ppermute | solution.py:611
  67.4 37.8 %all_to_all.10 = bf16[128,8,128]{2,1,0:T(8,128)(2,1)S(1)} all-to-all(bf16[128,8,128]{2,1,0:T(8,128)(2,1)S(1)} %fusion.1), channel_id=1, replica_groups=mesh['row'=8,'col_half'=16,'core'=2] {'row','col_half'}, dimensions={0} | all-to-all | bytes 524288 | tf_op jit(solution)/shard_map/all_to_all | solution.py:614
  105.3 0.1 reduce_sum.12
  105.5 18.5 %all_to_all.11 = bf16[128,8,128]{2,1,0:T(8,128)(2,1)S(1)} all-to-all(bf16[128,8,128]{2,1,0:T(8,128)(2,1)S(1)} %broadcast_in_dim.2), channel_id=1, replica_groups=mesh['row'=8,'col_half'=16,'core'=2] {'row','col_half'}, dimensions={0} | all-to-all | bytes 524288 | tf_op jit(solution)/shard_map/all_to_all | solution.py:616
  124.0 3.6 %collective-permute-start.5 = (bf16[1024,128]{1,0:T(8,128)(2,1)S(1)}, bf16[1024,128]{1,0:T(8,128)(2,1)S(1)}, u32[]{:S(2)}, u32[]{:S(2)}) collective-permute-start(bf16[1024,128]{1,0:T(8,128)(2,1)S(1)} %bitcast.16), channel_id=1, source_target_pairs={{0,1},{1,0},{2,3},{3,2},{4,5},{5,4},{6,7},{7,6},{8,9},{9,8},{10,11... | collective-permute-start | bytes 786440 | tf_op jit(solution)/shard_map/ppermute | solution.py:618
  127.5 1.2 collective-permute-done.5.other
  128.7 0.7 copy-done.16
  129.4 2.0 %unpack.1 = (f32[2,2,96]{2,1,0:T(2,128)}, f32[2,96,288]{2,1,0:T(8,128)}, f32[2,288]{1,0:T(2,128)}, f32[3,2,225]{2,1,0:T(2,128)}, f32[2,96,96]{2,1,0:T(8,128)}, /...) custom-call(s32[4]{0:T(128)} %pad_add_fusion.place, bf16[1024,128]{1,0:T(8,128)(2,1)} %bitcast.17, ...), custom_call_target="tpu_custom_call" | custom-call | tf_op jit(solution)/shard_map/unpack/pallas_call | solution.py:619
  (33 shorter events, 0.2 us)
Async XLA Ops:
  1.3 24.4 %copy-start.8 = (bf16[2,384,96]{1,2,0:T(8,128)(2,1)S(1)}, bf16[2,384,96]{1,2,0:T(8,128)(2,1)}, u32[]{:S(2)}) copy-start(bf16[2,384,96]{1,2,0:T(8,128)(2,1)} %param.19) | copy-start | bytes 442372
  1.3 24.4 %copy-start.9 = (bf16[2,96,96]{2,1,0:T(8,128)(2,1)S(1)}, bf16[2,96,96]{2,1,0:T(8,128)(2,1)}, u32[]{:S(2)}) copy-start(bf16[2,96,96]{2,1,0:T(8,128)(2,1)} %proj_weight.1) | copy-start | bytes 110596
  3.1 11.0 %collective-permute-start = (bf16[12,48,96]{2,1,0:T(8,128)(2,1)}, bf16[12,48,96]{2,1,0:T(8,128)(2,1)S(1)}, u32[]{:S(2)}, u32[]{:S(2)}) collective-permute-start(bf16[12,48,96]{2,1,0:T(8,128)(2,1)} %get-tuple-element.25), channel_id=1, source_target_pairs={{0,32},{32,0},{64,96},{96,64},{128,160},{160,128},{192,224},{224,1... | collective-permute-start | bytes 331784 | tf_op jit(solution)/shard_map/ppermute | solution.py:574
  10.9 14.8 %copy-start = (bf16[16,48,96]{2,1,0:T(8,128)(2,1)S(1)}, bf16[16,48,96]{2,1,0:T(8,128)(2,1)}, u32[]{:S(2)}) copy-start(bf16[16,48,96]{2,1,0:T(8,128)(2,1)} %region.5) | copy-start | bytes 442372
  10.9 14.8 %copy-start.1 = (bf16[16,48,96]{2,1,0:T(8,128)(2,1)S(1)}, bf16[16,48,96]{2,1,0:T(8,128)(2,1)}, u32[]{:S(2)}) copy-start(bf16[16,48,96]{2,1,0:T(8,128)(2,1)} %cot.5) | copy-start | bytes 442372
  10.9 14.8 %copy-start.6 = (bf16[2,96,288]{2,1,0:T(8,128)(2,1)S(1)}, bf16[2,96,288]{2,1,0:T(8,128)(2,1)}, u32[]{:S(2)}) copy-start(bf16[2,96,288]{2,1,0:T(8,128)(2,1)} %qkv_weight.1) | copy-start | bytes 331780
  10.9 14.8 %copy-start.7 = (bf16[2,96,384]{2,1,0:T(8,128)(2,1)S(1)}, bf16[2,96,384]{2,1,0:T(8,128)(2,1)}, u32[]{:S(2)}) copy-start(bf16[2,96,384]{2,1,0:T(8,128)(2,1)} %up_weight.1) | copy-start | bytes 442372
  10.9 3.2 %collective-permute-start.1 = (bf16[12,48,96]{2,1,0:T(8,128)(2,1)}, bf16[12,48,96]{2,1,0:T(8,128)(2,1)S(1)}, u32[]{:S(2)}, u32[]{:S(2)}) collective-permute-start(bf16[12,48,96]{2,1,0:T(8,128)(2,1)} %get-tuple-element.26), channel_id=1, source_target_pairs={{32,64},{64,32},{96,128},{128,96},{160,192},{192,160},{33,65},{65,... | collective-permute-start | bytes 331784 | tf_op jit(solution)/shard_map/ppermute | solution.py:574
  14.1 0.7 copy-start.2
  14.8 0.7 copy-start.4
  15.4 10.3 %copy-start.13 = (f32[2,384]{1,0:T(2,128)S(1)}, f32[2,384]{1,0:T(2,128)}, u32[]{:S(2)}) copy-start(f32[2,384]{1,0:T(2,128)} %up_bias.1) | copy-start | bytes 9220
  15.4 10.3 %copy-start.14 = (f32[2,2,96]{2,1,0:T(2,128)S(1)}, f32[2,2,96]{2,1,0:T(2,128)}, u32[]{:S(2)}) copy-start(f32[2,2,96]{2,1,0:T(2,128)} %norm_gains.1) | copy-start | bytes 4612
  17.4 5.0 %collective-permute-start.2 = (bf16[56,8,96]{2,1,0:T(8,128)(2,1)}, bf16[56,8,96]{2,1,0:T(8,128)(2,1)S(1)}, u32[]{:S(2)}, u32[]{:S(2)}) collective-permute-start(bf16[56,8,96]{2,1,0:T(8,128)(2,1)} %get-tuple-element.27), channel_id=1, source_target_pairs={{0,1},{1,0},{2,3},{3,2},{4,5},{5,4},{6,7},{7,6},{8,9},{9,8},{10,11... | collective-permute-start | bytes 258056 | tf_op jit(solution)/shard_map/ppermute | solution.py:574
  19.3 6.5 %copy-start.11 = (f32[2,3,225]{2,0,1:T(2,128)S(1)}, f32[2,3,225]{2,0,1:T(2,128)}, u32[]{:S(2)}) copy-start(f32[2,3,225]{2,0,1:T(2,128)} %param.15) | copy-start | bytes 16204
  19.3 6.4 %collective-permute-start.3 = (bf16[56,8,96]{2,1,0:T(8,128)(2,1)}, bf16[56,8,96]{2,1,0:T(8,128)(2,1)S(1)}, u32[]{:S(2)}, u32[]{:S(2)}) collective-permute-start(bf16[56,8,96]{2,1,0:T(8,128)(2,1)} %get-tuple-element.28), channel_id=1, source_target_pairs={{1,2},{2,1},{3,4},{4,3},{5,6},{6,5},{7,8},{8,7},{9,10},{10,9},{11,... | collective-permute-start | bytes 258056 | tf_op jit(solution)/shard_map/ppermute | solution.py:574
  22.4 3.4 %copy-start.12 = (f32[2,288]{1,0:T(2,128)S(1)}, f32[2,288]{1,0:T(2,128)}, u32[]{:S(2)}) copy-start(f32[2,288]{1,0:T(2,128)} %qkv_bias.1) | copy-start | bytes 6916
  25.7 0.7 copy-start.10
  26.4 0.9 copy-start.3
  27.3 0.9 copy-start.5
  65.7 1.6 %collective-permute-start.4 = (bf16[1024,128]{1,0:T(8,128)(2,1)S(1)}, bf16[1024,128]{1,0:T(8,128)(2,1)S(1)}, u32[]{:S(2)}, u32[]{:S(2)}) collective-permute-start(bf16[1024,128]{1,0:T(8,128)(2,1)S(1)} %dynamic-slice_bitcast_fusion), channel_id=1, source_target_pairs={{0,1},{1,0},{2,3},{3,2},{4,5},{5,4},{6,7},{7,6},{8,9},{9,8},{10,11... | collective-permute-start | bytes 786440 | tf_op jit(solution)/shard_map/ppermute | solution.py:611
  124.0 4.7 %copy-start.15 = (bf16[128,8,128]{2,1,0:T(8,128)(2,1)}, bf16[128,8,128]{2,1,0:T(8,128)(2,1)S(1)}, u32[]{:S(2)}) copy-start(bf16[128,8,128]{2,1,0:T(8,128)(2,1)S(1)} %all_to_all.11) | copy-start | bytes 786436
  124.0 4.7 %collective-permute-start.5 = (bf16[1024,128]{1,0:T(8,128)(2,1)S(1)}, bf16[1024,128]{1,0:T(8,128)(2,1)S(1)}, u32[]{:S(2)}, u32[]{:S(2)}) collective-permute-start(bf16[1024,128]{1,0:T(8,128)(2,1)S(1)} %bitcast.16), channel_id=1, source_target_pairs={{0,1},{1,0},{2,3},{3,2},{4,5},{5,4},{6,7},{7,6},{8,9},{9,8},{10,11... | collective-permute-start | bytes 786440 | tf_op jit(solution)/shard_map/ppermute | solution.py:618
  128.7 0.7 copy-start.16

commit v2 on v1

v2 whole, which is shorter than its diff:
```python
import functools

import jax
import jax.numpy as jnp
from jax import lax
from jax.experimental import pallas as pl
from jax.experimental.pallas import tpu as pltpu
from jax.sharding import Mesh
from jax.sharding import PartitionSpec as P

C = 96
HEADS = 3
HEAD = 32
HID = 384
WIN = 8
TH = 16
TW = 48
AUG = 112
PAIR = 128
ROWS = 1024
PEERS = 128
LOG2E = 1.4426950408889634
SCALE = HEAD**-0.5
FAR = -1e30
F32 = jnp.float32
BF16 = jnp.bfloat16

LOWER = [(i, j) for i in (0, 1) for j in range(6)]
UPPER = LOWER + [(2, j) for j in range(7)] + [(0, 6), (1, 6)]
OWN_PAIRS = 6
UPPER_PAIRS = 11
CHUNK = 2
LIMIT = 60 * 1024 * 1024


def dot(a, b):
    return jnp.dot(a, b, preferred_element_type=F32)


def dot_nt(a, b):
    return lax.dot_general(a, b, (((1,), (1,)), ((), ())), preferred_element_type=F32)


def split3(v):
    hi = v.astype(BF16)
    rest = v - hi.astype(F32)
    mid = rest.astype(BF16)
    return hi, mid, (rest - mid.astype(F32)).astype(BF16)


def transposed(v):
    return jnp.transpose(v.astype(F32)).astype(BF16)


def augmented(weight, bias):
    hi, mid, lo = split3(bias)
    rows = lax.broadcasted_iota(jnp.int32, (AUG - C, bias.shape[1]), 0)
    extra = jnp.where(
        rows == 0,
        hi.astype(F32),
        jnp.where(rows == 1, mid.astype(F32), jnp.where(rows == 2, lo.astype(F32), 0.0)),
    )
    return transposed(jnp.concatenate([weight.astype(F32), extra], 0))


def lane_code(lanes):
    token = lanes % 64
    return (token // WIN) * 15 + token % WIN


def expand_table(row):
    parts = []
    for kr in range(WIN):
        wide = jnp.broadcast_to(row, (WIN, 256))
        parts.append(pltpu.roll(wide, (15 * kr - 112) % 256, 1, stride=1, stride_axis=0))
    rolled = jnp.concatenate(parts, 0)
    lane = lax.broadcasted_iota(jnp.int32, (256, PAIR), 0)
    query = lax.broadcasted_iota(jnp.int32, (256, PAIR), 1)
    onehot = (lane == lane_code(query)).astype(BF16)
    hi, mid, lo = split3(rolled)
    return (dot(hi, onehot) + dot(mid, onehot) + dot(lo, onehot)) * LOG2E


def fold_table(acc):
    lane = lax.broadcasted_iota(jnp.int32, (PAIR, 256), 1)
    query = lax.broadcasted_iota(jnp.int32, (PAIR, 256), 0)
    onehot = (lane == 112 - lane_code(query)).astype(BF16)
    hi, mid, _ = split3(acc)
    wide = dot(hi, onehot) + dot(mid, onehot)
    total = jnp.zeros((WIN, 256), F32)
    for kr in range(WIN):
        total += pltpu.roll(
            wide[kr * WIN : (kr + 1) * WIN], 15 * kr, 1, stride=1, stride_axis=0
        )
    return jnp.sum(total, 0, keepdims=True)


def reverse_lanes(rows):
    a = lax.broadcasted_iota(jnp.int32, (256, 256), 0)
    b = lax.broadcasted_iota(jnp.int32, (256, 256), 1)
    onehot = (a + b == 224).astype(BF16)
    hi, mid, _ = split3(rows)
    return dot(hi, onehot) + dot(mid, onehot)


def norm(x):
    mean = jnp.sum(x, 0, keepdims=True) * (1.0 / C)
    centred = x - mean
    var = jnp.sum(centred * centred, 0, keepdims=True) * (1.0 / C)
    r = lax.rsqrt(var + 1e-05)
    return centred * r, r


def norm_back(dxhat, xhat, r):
    m1 = jnp.sum(dxhat, 0, keepdims=True) * (1.0 / C)
    m2 = jnp.sum(dxhat * xhat, 0, keepdims=True) * (1.0 / C)
    return r * (dxhat - m1 - xhat * m2)


def per_pair(v):
    return [v[:, p : p + PAIR] for p in range(0, v.shape[1], PAIR)]


def per_heads(v):
    step = HEADS * PAIR
    return [v[:, p : p + step] for p in range(0, v.shape[1], step)]


def across(ref, start, count):
    return jnp.concatenate([ref[start + p] for p in range(count)], 1)


def keep_pairs(ref, start, v):
    for p, part in enumerate(per_pair(v)):
        ref[start + p] = part


def scaled(v, gain):
    return jnp.concatenate([part * gain for part in per_pair(v)], 1)


def with_ones(v):
    return jnp.concatenate([v, jnp.ones((AUG - C, v.shape[1]), BF16)], 0)


def head_blocks(v):
    zero = jnp.zeros((HEAD, PAIR), v.dtype)
    cols = []
    for h in range(HEADS):
        rows = [v[g * HEAD : (g + 1) * HEAD] if g == h else zero for g in range(HEADS)]
        cols.append(jnp.concatenate(rows, 0))
    return jnp.concatenate(cols, 1)


def first_lanes(v):
    lane = lax.broadcasted_iota(jnp.int32, (1, v.shape[1]), 1)
    return (lane % PAIR) < 64


def window_rows(v):
    zero = jnp.zeros_like(v)
    first = jnp.broadcast_to(first_lanes(v), v.shape)
    return jnp.concatenate([jnp.where(first, v, zero), jnp.where(first, zero, v)], 0)


def deep_rows(v):
    pad = jnp.zeros((PAIR - C, HEADS * PAIR), v.dtype)
    return window_rows(jnp.concatenate([head_blocks(v), pad], 0))


def deep_tokens(v):
    pad = jnp.zeros((PAIR - C, PAIR), v.dtype)
    tokens = transposed(jnp.concatenate([v, pad], 0))
    return jnp.concatenate([tokens[:64], tokens[64:]], 1)


def head_diagonal(v):
    return jnp.concatenate(
        [v[h * HEAD : (h + 1) * HEAD, h * PAIR : (h + 1) * PAIR] for h in range(HEADS)], 0
    )


def gelu_parts(u):
    k = 0.7978845608028654
    uu = u * u
    half = 0.5 + 0.5 * jnp.tanh(u * (k + (k * 0.044715) * uu))
    m = u * half
    return m, half + m * (1.0 - half) * (2 * k + (6 * k * 0.044715) * uu)


def forward(x, b, w, penalty, keep=lambda n, v: None):
    xhat1, r1 = norm(x)
    keep(0, xhat1)
    keep(1, r1)
    a = with_ones(scaled(xhat1, w.gain[b, 0]).astype(BF16))
    keep(2, a)
    qkv = dot(w.qkv_t[b], a).astype(BF16)
    keep(3, qkv)
    parts = per_pair(qkv)
    scores = [dot(deep_tokens(part[C : 2 * C]), deep_rows(part[:C])) for part in parts]
    probs = []
    for p in range(0, len(parts), CHUNK):
        some = range(p, min(p + CHUNK, len(parts)))
        bias = jnp.concatenate([w.bias[b]] * len(some), 1)
        score = jnp.concatenate([scores[q] for q in some], 1) * (SCALE * LOG2E) + bias
        if penalty is not None:
            none = jnp.zeros((64, PAIR), F32)
            extra = [none if penalty[q] is None else penalty[q] for q in some]
            score = score + jnp.concatenate([v for v in extra for _ in range(HEADS)], 1)
        e = jnp.exp2(score - jnp.max(score, 0, keepdims=True))
        probs.append((e * (1.0 / jnp.sum(e, 0, keepdims=True))).astype(BF16))
    probs = jnp.concatenate(probs, 1)
    keep(4, probs)
    mixed = [
        head_diagonal(dot(part[2 * C :], window_rows(prob)))
        for part, prob in zip(parts, per_heads(probs))
    ]
    mix = jnp.concatenate(mixed, 1).astype(BF16)
    keep(5, mix)
    h = x + dot(w.proj_t[b], mix)
    xhat2, r2 = norm(h)
    keep(6, xhat2)
    keep(7, r2)
    f = with_ones(scaled(xhat2, w.gain[b, 1]).astype(BF16))
    keep(8, f)
    u = dot(w.up_t[b], f)
    m, slope = gelu_parts(u)
    m = m.astype(BF16)
    keep(9, m)
    keep(10, slope)
    out = h + dot(w.down_t[b], m)
    return out, (xhat1, r1, a, qkv, probs, mix, xhat2, r2, f, m, slope)


def backward(g, b, w, saved, mask):
    xhat1, r1, a, qkv, probs, mix, xhat2, r2, f, m, slope = saved

    def own(v):
        return v if mask is None else v * mask.astype(v.dtype)

    def pairs_sum(v):
        return sum(per_pair(v))

    g16 = g.astype(BF16)
    du = (dot(w.down[b], g16) * slope).astype(BF16)
    w.d_down[b] += dot_nt(own(g16), m)
    w.d_up[b] += dot_nt(own(f), du)
    df = dot(w.up[b], du)
    w.d_gain[b, 1] += pairs_sum(own(df * xhat2))
    dh = g + norm_back(scaled(df, w.gain[b, 1]), xhat2, r2)
    dh16 = dh.astype(BF16)
    w.d_proj[b] += dot_nt(mix, own(dh16))
    dmix = dot(w.proj[b], dh16).astype(BF16)
    parts, d_parts = per_pair(qkv), per_pair(dmix)
    dprobs = [dot(deep_tokens(v[2 * C :]), deep_rows(d)) for v, d in zip(parts, d_parts)]
    ds16 = []
    d_bias = jnp.zeros((64, HEADS * PAIR), F32)
    for p in range(0, len(parts), CHUNK):
        some = range(p, min(p + CHUNK, len(parts)))
        prob = probs[:, HEADS * PAIR * p : HEADS * PAIR * (p + len(some))].astype(F32)
        weighted = prob * jnp.concatenate([dprobs[q] for q in some], 1)
        ds = weighted - prob * jnp.sum(weighted, 0, keepdims=True)
        ds16.append(ds.astype(BF16))
        for q, part in zip(some, per_heads(ds)):
            if mask is not None:
                part = part * jnp.concatenate([per_pair(mask)[q]] * HEADS, 1)
            d_bias = d_bias + part
    w.d_bias[b] += d_bias
    dq, dk, dv = [], [], []
    ds16 = jnp.concatenate(ds16, 1)
    for part, d_part, prob, ds in zip(parts, d_parts, per_heads(probs), per_heads(ds16)):
        ds = window_rows(ds)
        dv.append(dot_nt(head_blocks(d_part), window_rows(prob)))
        dk.append(dot_nt(head_blocks(part[:C]), ds) * SCALE)
        dq.append(head_diagonal(dot(part[C : 2 * C], ds)) * SCALE)
    dqkv = jnp.concatenate([jnp.concatenate(v, 1) for v in (dq, dk, dv)], 0).astype(BF16)
    w.d_qkv[b] += dot_nt(own(a), dqkv)
    da = dot(w.qkv[b], dqkv)
    w.d_gain[b, 0] += pairs_sum(own(da * xhat1))
    return dh + norm_back(scaled(da, w.gain[b, 0]), xhat1, r1)


class Layers:
    pass


class PerLayer:
    def __init__(self, *refs):
        self.refs = refs

    def __getitem__(self, key):
        if isinstance(key, tuple):
            return self.refs[key[0]][key[1]]
        return self.refs[key][...]


def fetch(pairs, sems):
    copies = [pltpu.make_async_copy(src, dst, sems.at[n]) for n, (src, dst) in enumerate(pairs)]
    for copy in copies:
        copy.start()
    return copies


def finish(copies):
    for copy in copies:
        copy.wait()


def windows_t(ref, places, r0, c0):
    tokens = []
    for i, j in places:
        block = ref[r0 + WIN * i : r0 + WIN * (i + 1), c0 + WIN * j : c0 + WIN * (j + 1), :]
        tokens.append(block.astype(F32).reshape(WIN * WIN, C))
    if len(tokens) == 1:
        tokens.append(jnp.zeros((WIN * WIN, C), F32))
    return jnp.transpose(jnp.concatenate(tokens, 0))


def windows_back(value, ref, places):
    tokens = jnp.transpose(value)
    for n, (i, j) in enumerate(places):
        block = tokens[n * 64 : (n + 1) * 64].reshape(WIN, WIN, C)
        ref[WIN * i : WIN * (i + 1), WIN * j : WIN * (j + 1), :] = block.astype(ref.dtype)


VMEM = pl.BlockSpec(memory_space=pltpu.VMEM)
HBM = pl.BlockSpec(memory_space=pltpu.HBM)
COL_AXES = ("col_half", "core")
SAVES = [
    ((OWN_PAIRS, C, PAIR), F32),
    ((OWN_PAIRS, 1, PAIR), F32),
    ((OWN_PAIRS, AUG, PAIR), BF16),
    ((OWN_PAIRS, 3 * C, PAIR), BF16),
    ((OWN_PAIRS, 64, HEADS * PAIR), BF16),
    ((OWN_PAIRS, C, PAIR), BF16),
    ((OWN_PAIRS, C, PAIR), F32),
    ((OWN_PAIRS, 1, PAIR), F32),
    ((OWN_PAIRS, AUG, PAIR), BF16),
    ((OWN_PAIRS, HID, PAIR), BF16),
    ((OWN_PAIRS, HID, PAIR), BF16),
]


def shapes(entries):
    return [jax.ShapeDtypeStruct(shape, kind) for shape, kind in entries]


def scratch(entries):
    return [pltpu.VMEM(shape, kind) for shape, kind in entries]


def sides(position, from_a, from_b):
    even = position % 2 == 0
    return jnp.where(even, from_b, from_a), jnp.where(even, from_a, from_b)


def to_sides(position, before, after):
    even = position % 2 == 0
    return jnp.where(even, after, before), jnp.where(even, before, after)


def wide_gains(norm_gains, b):
    rows = [jnp.broadcast_to(norm_gains[b, n : n + 1, :], (PAIR, C)) for n in range(2)]
    return [jnp.transpose(row) for row in rows]


def keep_bias(bias, table, bias_table, b):
    table[...] = jnp.zeros(table.shape, F32)
    for h in range(HEADS):
        table[h : h + 1, 0 : bias_table.shape[2]] = bias_table[h, b : b + 1, :]
        bias[:, h * PAIR : (h + 1) * PAIR] = expand_table(table[h : h + 1, :])


GAIN = ((2, C, PAIR), F32)
BIAS = ((64, HEADS * PAIR), F32)
QKV_T = ((3 * C, AUG), BF16)
PROJ_T = ((C, C), BF16)
UP_T = ((HID, AUG), BF16)
DOWN = ((HID, C), BF16)
TABLE = ((8, 256), F32)
SMALL = [((2, 2, C), F32), ((2, 3 * C), F32), ((HEADS, 2, 225), F32), ((2, HID), F32)]
WEIGHTS = [((2, C, 3 * C), BF16), ((2, C, C), BF16), ((2, C, HID), BF16), ((2, C, HID), BF16)]
FIRST = [((C, 3 * C), BF16), ((C, C), BF16), ((C, HID), BF16), ((C, HID), BF16)]
TILE = ((TH, TW, C), BF16)


def lower_kernel(
    region,
    cot,
    norm_gains,
    qkv_bias,
    bias_table,
    up_bias,
    qkv_weight,
    proj_weight,
    up_weight,
    down_t,
    low_far,
    far_a,
    far_b,
    *rest,
):
    saves, rest = rest[: len(SAVES)], rest[len(SAVES) :]
    sems, field, table, gain, bias, tile, cot_tile, low, send_a, send_b, *rest = rest
    small, weights, kept = rest[:4], rest[4:8], rest[8:]
    sources = [norm_gains, qkv_bias, bias_table, up_bias]
    sources += [ref.at[0] for ref in (qkv_weight, proj_weight, up_weight, down_t)]
    copies = fetch(zip(sources + [region, cot], small + weights + [tile, cot_tile]), sems)
    w = Layers()
    finish(copies[:8])
    norm_gains, qkv_bias, bias_table, up_bias = small
    gain[0], gain[1] = wide_gains(norm_gains, 0)
    keep_bias(bias, table, bias_table, 0)
    w.gain, w.bias, w.down_t = PerLayer(gain), PerLayer(bias), PerLayer(weights[3])
    w.qkv_t = [augmented(weights[0][...], qkv_bias[0:1, :])]
    w.proj_t = [transposed(weights[1][...])]
    w.up_t = [augmented(weights[2][...], up_bias[0:1, :])]
    finish(copies[8:])
    x = [windows_t(tile, LOWER[2 * n : 2 * n + 2], 0, 0) for n in range(OWN_PAIRS)]
    leaving = []

    def keep(k, value):
        ref = kept[k]
        parts = per_heads(value) if ref.shape[2] == HEADS * PAIR else per_pair(value)
        for n, part in enumerate(parts):
            ref[n] = part.astype(ref.dtype)
        leaving.append(pltpu.make_async_copy(ref, saves[k], sems.at[13 + k]))
        leaving[-1].start()

    y, _ = forward(jnp.concatenate(x, 1), 0, w, None, keep)
    for n, part in enumerate(per_pair(y)):
        windows_back(part, field, LOWER[2 * n : 2 * n + 2])
    value = field[...].astype(BF16)
    low[...] = value
    top = jnp.concatenate([value[0:4], cot_tile[0:4]], 0)
    bottom = jnp.concatenate([value[TH - 4 :], cot_tile[TH - 4 :]], 0)
    near_part, far_part = to_sides(lax.axis_index("row"), top, bottom)
    send_a[...] = near_part
    send_b[...] = far_part
    leaving += fetch([(low, low_far), (send_a, far_a), (send_b, far_b)], sems.at[pl.ds(10, 3)])
    finish(leaving)


def prepare_kernel(
    after,
    norm_gains,
    qkv_bias,
    bias_table,
    up_bias,
    qkv_weight,
    proj_weight,
    up_weight,
    down_t,
    *rest,
):
    far, (sems, table), rest = rest[:8], rest[8:10], rest[10:]
    (qkv, proj, up, down_copy), small, made = rest[:4], rest[4:8], rest[8:]
    gain_0, gain_1, bias, qkv_t, proj_t, up_t, down_0, down_1 = made
    sources = [norm_gains, qkv_bias, bias_table, up_bias]
    sources += [qkv_weight, proj_weight, up_weight, down_t]
    finish(fetch(zip(sources, list(small) + [qkv, proj, up, down_copy]), sems))
    norm_gains, qkv_bias, bias_table, up_bias = small
    for b, gain in enumerate((gain_0, gain_1)):
        gain[0], gain[1] = wide_gains(norm_gains, b)
    keep_bias(bias, table, bias_table, 1)
    qkv_t[...] = augmented(qkv[1], qkv_bias[1:2, :])
    proj_t[...] = transposed(proj[1])
    up_t[...] = augmented(up[1], up_bias[1:2, :])
    down_0[...] = transposed(down_copy[0])
    down_1[...] = transposed(down_copy[1])
    finish(fetch(zip(made, far), sems))


PREPARED = [GAIN, GAIN, BIAS, QKV_T, PROJ_T, UP_T, DOWN, DOWN]


def strip_kernel(*refs):
    sources, (far_a, far_b, sems, send_a, send_b), places = refs[:4], refs[4:9], refs[9:]
    finish(fetch(zip(sources, places), sems))
    row = lax.axis_index("row")
    both = []
    for cols in (slice(0, 8), slice(TW - 8, TW)):
        strips = []
        for n, own in enumerate(places[:2]):
            above, below = sides(row, places[2][4 * n : 4 * n + 4], places[3][4 * n : 4 * n + 4])
            tall = [v.astype(F32) for v in (above[:, cols], own[:, cols], below[:, cols])]
            tall = jnp.concatenate(tall, 0)
            half = tall[:, 0:4] if cols.start == 0 else tall[:, 4:8]
            strips.append(jnp.concatenate([half[0:12], half[12:24]], 1))
        both.append(jnp.concatenate(strips, 0).astype(BF16))
    near_part, far_part = to_sides(lax.axis_index(COL_AXES), *both)
    send_a[...] = near_part
    send_b[...] = far_part
    finish(fetch([(send_a, far_a), (send_b, far_b)], sems))


UPPER_IN = [TILE, TILE] + [((8, TW, C), BF16)] * 2 + [((24, 8, C), BF16)] * 2
UPPER_IN += WEIGHTS + PREPARED + SAVES


def upper_kernel(rows_cols, *rest):
    sources, rest = rest[: len(UPPER_IN)], rest[len(UPPER_IN) :]
    out_far, grad_far, keep_far, give_far, sems, out, grad_region, packed, *rest = rest
    local_in, rest = rest[: len(UPPER_IN)], rest[len(UPPER_IN) :]
    low_field, cot_field, out_field, grad_field, table, misc, *rest = rest
    d_gain, d_qkv, d_proj, d_up, d_down, d_bias = rest
    copies = fetch(zip(sources, local_in), sems)
    low, cot_tile = local_in[:2]
    got_row, got_col = local_in[2:4], local_in[4:6]
    prepared, saves = local_in[10:18], local_in[18:]

    w = Layers()
    w.qkv, w.proj, w.up, w.down_t = local_in[6:10]
    w.gain = PerLayer(*prepared[:2])
    w.bias, w.qkv_t, w.proj_t, w.up_t = [PerLayer(None, ref) for ref in prepared[2:6]]
    w.down = PerLayer(*prepared[6:])
    w.d_gain, w.d_qkv, w.d_proj = d_gain, d_qkv, d_proj
    w.d_up, w.d_down, w.d_bias = d_up, d_down, d_bias
    row, col = lax.axis_index("row"), lax.axis_index(COL_AXES)
    first_row, last_row = row == 0, row == rows_cols[0] - 1
    first_col, last_col = col == 0, col == rows_cols[1] - 1

    for ref in (d_gain, d_qkv, d_proj, d_up, d_down, d_bias, misc):
        ref[...] = jnp.zeros(ref.shape, F32)
    table[...] = jnp.zeros(table.shape, F32)
    finish(copies[:6])
    left, right = sides(col, got_col[0][...].astype(F32), got_col[1][...].astype(F32))
    inner = slice(8, 8 + TW)
    for n, (field, own) in enumerate(((low_field, low), (cot_field, cot_tile))):
        part = slice(4 * n, 4 * n + 4)
        above, below = sides(row, got_row[0][part], got_row[1][part])
        field[0:4, inner, :] = above.astype(F32)
        field[4 : 4 + TH, inner, :] = own[...].astype(F32)
        field[4 + TH :, inner, :] = below.astype(F32)
        for half in range(2):
            rows = slice(12 * half, 12 * half + 12)
            from_rows, from_cols = slice(12 * n, 12 * n + 12), slice(4 * half, 4 * half + 4)
            field[rows, 4:8, :] = left[from_rows, from_cols, :]
            field[rows, 8 + TW : 12 + TW, :] = right[from_rows, from_cols, :]

    def edges(s):
        i, j = UPPER[s] if s < len(UPPER) else (1, 1)
        flags = (first_row, i == 0), (last_row, i == 2), (first_col, j == 0), (last_col, j == 6)
        return [jnp.where(flag, FAR, 0.0) if here else 0.0 for flag, here in flags]

    places = [UPPER[2 * n : 2 * n + 2] for n in range(UPPER_PAIRS)]
    key = lax.broadcasted_iota(jnp.int32, (64, PAIR), 0)
    first = lax.broadcasted_iota(jnp.int32, (64, PAIR), 1) < 64
    upper_half = (key // WIN) < 4
    left_half = (key % WIN) < 4
    penalty = []
    for n in range(UPPER_PAIRS):
        one, two = edges(2 * n), edges(2 * n + 1)
        if all(i == 1 and 0 < j < 6 for i, j in places[n]):
            penalty.append(None)
            continue
        top, bottom, before, after = [jnp.where(first, v, u) for v, u in zip(one, two)]
        penalty.append(jnp.where(upper_half, top, bottom) + jnp.where(left_half, before, after))
    slot = lax.broadcasted_iota(jnp.int32, (1, UPPER_PAIRS * PAIR), 1) // 64
    row_own = jnp.where(last_row, 1.0, 0.0)
    col_own = jnp.where(last_col, 1.0, 0.0)
    mask = jnp.where(
        slot < 12,
        1.0,
        jnp.where(
            slot < 18,
            row_own,
            jnp.where(slot < 19, row_own * col_own, jnp.where(slot < 21, col_own, 0.0)),
        ),
    )

    finish(copies[6:18])
    x = jnp.concatenate([windows_t(low_field, p, 0, 4) for p in places], 1)
    g = jnp.concatenate([windows_t(cot_field, p, 0, 4) for p in places], 1)
    y, saved = forward(x, 1, w, penalty)
    for p, part in zip(places, per_pair(y)):
        windows_back(part, out_field, p)
    out[...] = out_field[4 : 4 + TH, 4 : 4 + TW, :].astype(BF16)
    leaving = fetch([(out, out_far)], sems)
    dx = backward(g, 1, w, saved, mask)
    for p, part in zip(places, per_pair(dx)):
        windows_back(part, grad_field, p)

    g = jnp.concatenate([windows_t(grad_field, p, 4, 4) for p in places[:OWN_PAIRS]], 1)
    finish(copies[18:])
    saved = [jnp.concatenate([ref[n] for n in range(OWN_PAIRS)], 1) for ref in saves]
    dx = backward(g, 0, w, saved, None)
    for p, part in zip(places, per_pair(dx)):
        windows_back(part, grad_region, p)
    leaving += fetch([(grad_region, grad_far)], sems.at[pl.ds(1, 1)])

    for b in range(2):
        for j in range(3):
            lanes = slice(j * PAIR, (j + 1) * PAIR)
            packed[b, j * C : (j + 1) * C, :] = d_up[b, 0:C, lanes].astype(BF16)
            packed[b, 288 + j * C : 288 + (j + 1) * C, :] = d_down[b, :, lanes].astype(BF16)
            misc[b, 3 + j : 4 + j, :] = d_up[b, C : C + 1, lanes]
        for j in range(2):
            lanes = slice(j * PAIR, (j + 1) * PAIR)
            packed[b, 576 + j * C : 576 + (j + 1) * C, :] = d_qkv[b, 0:C, lanes].astype(BF16)
            misc[b, j : j + 1, :] = d_qkv[b, C : C + 1, lanes]
        last = jnp.concatenate([d_qkv[b, 0:C, 256:288], d_proj[b]], 1)
        packed[b, 768:864, :] = last.astype(BF16)
        misc[b, 2:3, 0:32] = d_qkv[b, C : C + 1, 256:288]
        for n in range(2):
            column = jnp.sum(jnp.transpose(d_gain[b, n]), 0, keepdims=True)
            misc[b, 6 + n : 7 + n, 0:C] = column
        for h in range(HEADS):
            table[h : h + 1, :] = fold_table(d_bias[b, :, h * PAIR : (h + 1) * PAIR])
        rows = reverse_lanes(table[...])
        misc[b, 8:16, :] = rows[:, 0:PAIR]
        misc[b, 16:24, :] = rows[:, PAIR:]
        packed[b, 864:896, :] = misc[b].astype(BF16)
        packed[b, 896:ROWS, :] = jnp.zeros((ROWS - 896, PAIR), BF16)
    core = lax.axis_index("core")
    pairs = [(packed.at[core], keep_far), (packed.at[1 - core], give_far)]
    finish(leaving + fetch(pairs, sems.at[pl.ds(2, 2)]))


def unpack_kernel(
    mine_far, other_far, gains, qkv, qkv_bias, table, proj, up, up_bias, down_t, sems, mine, other
):
    finish(fetch([(mine_far, mine), (other_far, other)], sems))
    core = lax.axis_index("core")
    for b in range(2):
        flat = jnp.where(core == b, mine[...], other[...]).astype(F32)
        misc = flat[864:896]
        for j in range(3):
            lanes = slice(j * PAIR, (j + 1) * PAIR)
            up[b, :, lanes] = flat[j * C : (j + 1) * C]
            down_t[b, :, lanes] = flat[288 + j * C : 288 + (j + 1) * C]
            up_bias[b : b + 1, lanes] = misc[3 + j : 4 + j]
        for j in range(2):
            lanes = slice(j * PAIR, (j + 1) * PAIR)
            qkv[b, :, lanes] = flat[576 + j * C : 576 + (j + 1) * C]
            qkv_bias[b : b + 1, lanes] = misc[j : j + 1]
        last = flat[768:864]
        qkv[b, :, 256:288] = last[:, 0:32]
        proj[b] = last[:, 32:PAIR]
        qkv_bias[b : b + 1, 256:288] = misc[2:3, 0:32]
        for n in range(2):
            gains[b, n : n + 1, :] = misc[6 + n : 7 + n, 0:C]
        for h in range(HEADS):
            table[h, b : b + 1, 0:PAIR] = misc[8 + h : 9 + h]
            table[h, b : b + 1, PAIR:225] = misc[16 + h : 17 + h, 0:97]


def near(count):
    return [(i, i ^ 1) for i in range(count)]


def far(count):
    return [(i, ((i - 1) ^ 1) + 1) for i in range(1, count - 1)]


def swap(pair, axes, count):
    return lax.ppermute(pair[0], axes, near(count)), lax.ppermute(pair[1], axes, far(count))


def body(region, cotangent, gains, qkv, qkv_bias, table, proj, up, up_bias, down):
    rows, cols = lax.axis_size("row"), lax.axis_size(COL_AXES)
    table_t = jnp.transpose(table, (1, 0, 2))
    down_t = jnp.transpose(down, (0, 2, 1))
    params = (gains, qkv_bias, table_t, up_bias, qkv, proj, up, down_t)
    limit = pltpu.CompilerParams(vmem_limit_bytes=LIMIT)

    def dma(count):
        return [pltpu.SemaphoreType.DMA((count,))]

    strip = ((8, TW, C), BF16)
    low, send_a, send_b, *saved = pl.pallas_call(
        lower_kernel,
        out_shape=shapes([TILE, strip, strip] + SAVES),
        in_specs=[HBM] * 10,
        out_specs=[HBM] * (3 + len(SAVES)),
        scratch_shapes=dma(13 + len(SAVES))
        + scratch([((TH, TW, C), F32), TABLE, GAIN, BIAS, TILE, TILE, TILE, strip, strip])
        + scratch(SMALL + FIRST + SAVES),
        compiler_params=limit,
        name="lower",
    )(region, cotangent, *params)
    row_got = swap((send_a, send_b), "row", rows)
    prepared = pl.pallas_call(
        prepare_kernel,
        out_shape=shapes(PREPARED),
        in_specs=[HBM] * 9,
        out_specs=[HBM] * len(PREPARED),
        scratch_shapes=dma(8) + scratch([TABLE] + WEIGHTS + SMALL + PREPARED),
        compiler_params=limit,
        cost_estimate=pl.CostEstimate(flops=10**9, bytes_accessed=4 * 10**6, transcendentals=0),
        name="prepare",
    )(saved[1], *params)
    strip = ((24, 8, C), BF16)
    send = pl.pallas_call(
        strip_kernel,
        out_shape=shapes([strip, strip]),
        in_specs=[HBM] * 4,
        out_specs=[HBM] * 2,
        scratch_shapes=dma(4) + scratch([strip, strip] + UPPER_IN[:4]),
        compiler_params=limit,
        name="strips",
    )(low, cotangent, *row_got)
    col_got = swap(send, COL_AXES, cols)
    wide = ((TH + 8, TW + 16, C), F32)
    narrow = ((TH + 8, TW + 8, C), F32)
    sums = [
        ((2, 2, C, PAIR), F32),
        ((2, AUG, 3 * C), F32),
        ((2, C, C), F32),
        ((2, AUG, HID), F32),
        ((2, C, HID), F32),
        ((2, 64, HEADS * PAIR), F32),
    ]
    results = [TILE, ((TH, TW, C), F32)]
    flat = ((ROWS, PAIR), BF16)
    out, grad_region, keep, give = pl.pallas_call(
        functools.partial(upper_kernel, (rows, cols)),
        out_shape=shapes(results + [flat, flat]),
        in_specs=[HBM] * len(UPPER_IN),
        out_specs=[HBM] * 4,
        scratch_shapes=dma(len(UPPER_IN))
        + scratch(results + [((2, ROWS, PAIR), BF16)] + UPPER_IN + [wide, wide, narrow, narrow, TABLE, ((2, 32, PAIR), F32)] + sums),
        compiler_params=limit,
        name="upper",
    )(low, cotangent, *row_got, *col_got, qkv, proj, up, down_t, *prepared, *saved)
    got = lax.ppermute(give, "core", near(2))
    share = (keep.astype(F32) + got.astype(F32)).astype(BF16).reshape(PEERS, -1, PAIR)
    peers = ("row", "col_half")
    parts = lax.all_to_all(share, peers, 0, 0)
    part = jnp.sum(parts.astype(F32), 0, keepdims=True).astype(BF16)
    mine = lax.all_to_all(jnp.broadcast_to(part, share.shape), peers, 0, 0)
    mine = mine.reshape(ROWS, PAIR)
    other = lax.ppermute(mine, "core", near(2))
    grads = pl.pallas_call(
        unpack_kernel,
        out_shape=tuple(
            jax.ShapeDtypeStruct(shape, F32)
            for shape in (
                (2, 2, C),
                (2, C, 3 * C),
                (2, 3 * C),
                (HEADS, 2, 225),
                (2, C, C),
                (2, C, HID),
                (2, HID),
                (2, C, HID),
            )
        ),
        in_specs=[HBM] * 2,
        out_specs=[VMEM] * 8,
        scratch_shapes=dma(2) + scratch([flat, flat]),
        compiler_params=limit,
        name="unpack",
    )(mine, other)
    d_gains, d_qkv, d_qkv_bias, d_table, d_proj, d_up, d_up_bias, d_down_t = grads
    return (
        out,
        grad_region,
        d_gains,
        d_qkv,
        d_qkv_bias,
        jnp.transpose(d_table, (1, 0, 2)),
        d_proj,
        d_up,
        d_up_bias,
        jnp.transpose(d_down_t, (0, 2, 1)),
    )


def solution(mesh):
    rows, cols = mesh.devices.shape
    fine = Mesh(mesh.devices.reshape(rows, cols // 2, 2), ("row", "col_half", "core"))
    tile = P("row", ("col_half", "core"), None)
    return jax.shard_map(
        body,
        mesh=fine,
        in_specs=(tile, tile) + (P(),) * 8,
        out_specs=(tile, tile) + (P(),) * 8,
        check_vma=False,
    )
```

time: 132 us -> 103 us (0.78)
  Pallas kernels: 43.3 us -> 22.6 us
  waiting for transfers between devices: 8.38 us -> 4.8 us
  blocking collectives: 56.4 us -> 53.7 us
  local copies, waits for them, and re-layouts: 4.52 us -> 2.04 us
    pallas_call x3 -> x4, Pallas kernels: 41.3 us -> 20.5 us  [the longest x1 11.9 us: body(): pl.pallas_call(functools.partial(upper_kernel, (rows, cols)), out_shape=s...]
    ppermute x2, waiting for transfers between devices: 3.28 us -> 0.25 us  [swap(): lax.ppermute(pair[1], axes, far(count))]
    all_to_all x1, blocking collectives: 37.8 us -> 35.2 us  [body(): parts = lax.all_to_all(share, peers, 0, 0)]
    unnamed x34 -> x12, local copies, waits for them, and re-layouts: 4.47 us -> 2.01 us
  transfers between devices with their start and end apart: 6 -> 6, of which waited for: 4 -> 4; matrix products, arithmetic and copies ran while one was open for 0% -> 0% of each run, Pallas kernels for 0% -> 2%
where the time goes in v2:
time: 103 us; the launch traced here: 102 us
  blocking collectives  53.7 us (52%)
  Pallas kernels  22.6 us (22%)
  starting transfers between devices  17.2 us (17%)
  waiting for transfers between devices  4.8 us (5%)
  local copies, waits for them, and re-layouts  2.04 us (2%)
  other arithmetic  1.16 us (1%)
    all_to_all x1, blocking collectives, body(): parts = lax.all_to_all(share, peers, 0, 0)  35.2 us
    all_to_all x1, blocking collectives, body(): mine = lax.all_to_all(jnp.broadcast_to(part, share.shape), peers, 0, 0)  18.5 us
    pallas_call x1, Pallas kernels, body(): pl.pallas_call(functools.partial(upper_kernel, (rows, cols)), out_shape=s...  11.9 us
    ppermute x2, starting transfers between devices, swap(): lax.ppermute(pair[0], axes, near(count))  9.84 us
    pallas_call x1, Pallas kernels, body(): pl.pallas_call(lower_kernel, out_shape=shapes([TILE, strip, strip] + SAVE...  4.45 us
    ppermute x2, starting transfers between devices, swap(): lax.ppermute(pair[1], axes, far(count))  3.67 us
    ppermute x1, starting transfers between devices, body(): other = lax.ppermute(mine, 'core', near(2))  3.56 us
    pallas_call x1, Pallas kernels, body(): pl.pallas_call(prepare_kernel, out_shape=shapes(PREPARED), in_specs=[HBM]...  2.31 us
  transfers between devices with their start and end apart: 6, of which 4 were waited for; matrix products, arithmetic and copies ran while one was open for 0% of the time, Pallas kernels for 2%

profile of v2, /device:TPU:1, one launch (start us, length us, event | category | flops | bytes accessed | tf_op | source)
XLA Modules:
  0.0 102.3 jit_solution(15446055460309572322)
XLA Ops:
  0.6 4.5 %lower.1 = (bf16[16,48,96]{2,1,0:T(8,128)(2,1)}, bf16[8,48,96]{2,1,0:T(8,128)(2,1)}, bf16[8,48,96]{2,1,0:T(8,128)(2,1)}, f32[6,96,128]{2,1,0:T(8,128)}, f32[6,1,...) custom-call(bf16[16,48,96]{2,1,0:T(8,128)(2,1)} %region.1, ...), custom_call_target="tpu_custom_call" | custom-call | tf_op jit(solution)/shard_map/lower/pallas_call | solution.py:671
  5.1 7.8 %collective-permute-start = (bf16[8,48,96]{2,1,0:T(8,128)(2,1)}, bf16[8,48,96]{2,1,0:T(8,128)(2,1)S(1)}, u32[]{:S(2)}, u32[]{:S(2)}) collective-permute-start(bf16[8,48,96]{2,1,0:T(8,128)(2,1)} %get-tuple-element.47), channel_id=1, source_target_pairs={{0,32},{32,0},{64,96},{96,64},{128,160},{160,128},{192,224},{224,1... | collective-permute-start | bytes 221192 | tf_op jit(solution)/shard_map/ppermute | solution.py:657
  12.9 0.7 collective-permute-start.1
  13.6 1.7 %collective-permute-done.refs_2_.rest_2_ = bf16[8,48,96]{2,1,0:T(8,128)(2,1)S(1)} collective-permute-done((bf16[8,48,96]{2,1,0:T(8,128)(2,1)}, bf16[8,48,96]{2,1,0:T(8,128)(2,1)S(1)}, u32[]{:S(2)}, u32[]{:S(2)}) %collective-permute-start) | collective-permute-done | bytes 73760 | tf_op jit(solution)/shard_map/ppermute | solution.py:657
  15.3 0.6 copy-done.1
  15.9 0.0 copy-done.2
  15.9 1.8 %strips.1 = (bf16[24,8,96]{2,1,0:T(8,128)(2,1)}, bf16[24,8,96]{2,1,0:T(8,128)(2,1)}) custom-call(bf16[16,48,96]{2,1,0:T(8,128)(2,1)} %get-tuple-element.46.refs_0_.rest_0_, bf16[16,48,96]{2,1,0:T(8,128)(2,1)} %rest_1_.1, bf16[8,48,96]{2,1,0:T(8,128)(2,1)} %copy-done.1, bf16[8,48,96]{2,1,0:T(8,128)(2,1)} %copy-done.2), custom_call_target="tpu_custom_call" | custom-call | tf_op jit(solution)/shard_map/strips/pallas_call | solution.py:694
  17.8 2.0 %collective-permute-start.2 = (bf16[24,8,96]{2,1,0:T(8,128)(2,1)}, bf16[24,8,96]{2,1,0:T(8,128)(2,1)S(1)}, u32[]{:S(2)}, u32[]{:S(2)}) collective-permute-start(bf16[24,8,96]{2,1,0:T(8,128)(2,1)} %get-tuple-element.49), channel_id=1, source_target_pairs={{0,1},{1,0},{2,3},{3,2},{4,5},{5,4},{6,7},{7,6},{8,9},{9,8},{10,11... | collective-permute-start | bytes 110600 | tf_op jit(solution)/shard_map/ppermute | solution.py:657
  19.8 3.0 %collective-permute-start.3 = (bf16[24,8,96]{2,1,0:T(8,128)(2,1)}, bf16[24,8,96]{2,1,0:T(8,128)(2,1)S(1)}, u32[]{:S(2)}, u32[]{:S(2)}) collective-permute-start(bf16[24,8,96]{2,1,0:T(8,128)(2,1)} %get-tuple-element.50), channel_id=1, source_target_pairs={{1,2},{2,1},{3,4},{4,3},{5,6},{6,5},{7,8},{8,7},{9,10},{10,9},{11,... | collective-permute-start | bytes 110600 | tf_op jit(solution)/shard_map/ppermute | solution.py:657
  22.8 2.3 %prepare.1 = (f32[2,96,128]{2,1,0:T(8,128)}, f32[2,96,128]{2,1,0:T(8,128)}, f32[64,384]{1,0:T(8,128)}, bf16[288,112]{1,0:T(8,128)(2,1)}, bf16[96,96]{1,0:T(8,128...) custom-call(f32[6,1,128]{2,1,0:T(1,128)} %get-tuple-element.51.after.rest_19_, ...), custom_call_target="tpu_custom_call" | custom-call | flops 1000000000 | bytes 4000000 | tf_op jit(solution)/shard_map/prepare/pallas_call | solution.py:683
  25.1 0.2 collective-permute-done.3.rest_5_
  25.4 0.4 copy-done.4
  25.8 0.3 copy-done.5
  26.0 11.9 %upper.1 = (bf16[16,48,96]{2,1,0:T(8,128)(2,1)}, f32[16,48,96]{2,1,0:T(8,128)}, bf16[1024,128]{1,0:T(8,128)(2,1)}, bf16[1024,128]{1,0:T(8,128)(2,1)}) custom-call(bf16[16,48,96]{2,1,0:T(8,128)(2,1)} %get-tuple-element.46.refs_0_.rest_0_, bf16[16,48,96]{2,1,0:T(8,128)(2,1)} %rest_1_.1, bf16[8,48,96]{2,1,0:T(8,128)(2,1)} %copy-done.1, ...), custom_call_target="tpu_custom_call" | custom-call | tf_op jit(solution)/shard_map/upper/pallas_call | solution.py:716
  38.0 0.1 collective-permute-start.4
  38.1 1.7 %collective-permute-done.4 = bf16[1024,128]{1,0:T(8,128)(2,1)S(1)} collective-permute-done((bf16[1024,128]{1,0:T(8,128)(2,1)}, bf16[1024,128]{1,0:T(8,128)(2,1)S(1)}, u32[]{:S(2)}, u32[]{:S(2)}) %collective-permute-start.4) | collective-permute-done | bytes 262176 | tf_op jit(solution)/shard_map/ppermute | solution.py:726
  39.8 1.0 %fusion = bf16[128,8,128]{2,1,0:T(8,128)(2,1)S(1)} fusion(bf16[1024,128]{1,0:T(8,128)(2,1)S(1)} %collective-permute-done.4, bf16[1024,128]{1,0:T(8,128)(2,1)} %get-tuple-element.72), kind=kLoop, calls=%fused_computation.1 | loop fusion | flops 524288 | bytes 786432 | tf_op jit(solution)/shard_map/reshape | solution.py:727
  40.8 35.2 %all_to_all.10 = bf16[128,8,128]{2,1,0:T(8,128)(2,1)S(1)} all-to-all(bf16[128,8,128]{2,1,0:T(8,128)(2,1)S(1)} %fusion), channel_id=1, replica_groups=mesh['row'=8,'col_half'=16,'core'=2] {'row','col_half'}, dimensions={0} | all-to-all | bytes 524288 | tf_op jit(solution)/shard_map/all_to_all | solution.py:729
  76.0 0.1 reduce_sum.12
  76.2 18.5 %all_to_all.11 = bf16[128,8,128]{2,1,0:T(8,128)(2,1)S(1)} all-to-all(bf16[128,8,128]{2,1,0:T(8,128)(2,1)S(1)} %broadcast_in_dim.2), channel_id=1, replica_groups=mesh['row'=8,'col_half'=16,'core'=2] {'row','col_half'}, dimensions={0} | all-to-all | bytes 524288 | tf_op jit(solution)/shard_map/all_to_all | solution.py:731
  94.7 3.6 %collective-permute-start.5 = (bf16[1024,128]{1,0:T(8,128)(2,1)S(1)}, bf16[1024,128]{1,0:T(8,128)(2,1)S(1)}, u32[]{:S(2)}, u32[]{:S(2)}) collective-permute-start(bf16[1024,128]{1,0:T(8,128)(2,1)S(1)} %bitcast.7), channel_id=1, source_target_pairs={{0,1},{1,0},{2,3},{3,2},{4,5},{5,4},{6,7},{7,6},{8,9},{9,8},{10,11... | collective-permute-start | bytes 786440 | tf_op jit(solution)/shard_map/ppermute | solution.py:733
  98.3 1.2 %collective-permute-done.5.other_far = bf16[1024,128]{1,0:T(8,128)(2,1)S(1)} collective-permute-done((bf16[1024,128]{1,0:T(8,128)(2,1)S(1)}, bf16[1024,128]{1,0:T(8,128)(2,1)S(1)}, u32[]{:S(2)}, u32[]{:S(2)}) %collective-permute-start.5) | collective-permute-done | bytes 262176 | tf_op jit(solution)/shard_map/ppermute | solution.py:733
  99.4 0.7 copy-done.3
  100.1 2.0 %unpack.1 = (f32[2,2,96]{2,1,0:T(2,128)}, f32[2,96,288]{2,1,0:T(8,128)}, f32[2,288]{1,0:T(2,128)}, f32[3,2,225]{2,1,0:T(2,128)}, f32[2,96,96]{2,1,0:T(8,128)}, /...) custom-call(bf16[1024,128]{1,0:T(8,128)(2,1)} %bitcast.8, bf16[1024,128]{1,0:T(8,128)(2,1)} %copy-done.3), custom_call_target="tpu_custom_call" | custom-call | tf_op jit(solution)/shard_map/unpack/pallas_call | solution.py:734
  (10 shorter events, 0.1 us)
Async XLA Ops:
  5.1 10.1 %collective-permute-start = (bf16[8,48,96]{2,1,0:T(8,128)(2,1)}, bf16[8,48,96]{2,1,0:T(8,128)(2,1)S(1)}, u32[]{:S(2)}, u32[]{:S(2)}) collective-permute-start(bf16[8,48,96]{2,1,0:T(8,128)(2,1)} %get-tuple-element.47), channel_id=1, source_target_pairs={{0,32},{32,0},{64,96},{96,64},{128,160},{160,128},{192,224},{224,1... | collective-permute-start | bytes 221192 | tf_op jit(solution)/shard_map/ppermute | solution.py:657
  12.9 2.3 %collective-permute-start.1 = (bf16[8,48,96]{2,1,0:T(8,128)(2,1)}, bf16[8,48,96]{2,1,0:T(8,128)(2,1)S(1)}, u32[]{:S(2)}, u32[]{:S(2)}) collective-permute-start(bf16[8,48,96]{2,1,0:T(8,128)(2,1)} %get-tuple-element.48), channel_id=1, source_target_pairs={{32,64},{64,32},{96,128},{128,96},{160,192},{192,160},{33,65},{65,... | collective-permute-start | bytes 221192 | tf_op jit(solution)/shard_map/ppermute | solution.py:657
  15.2 0.6 copy-start.1
  15.3 0.7 copy-start.2
  17.8 7.4 %collective-permute-start.2 = (bf16[24,8,96]{2,1,0:T(8,128)(2,1)}, bf16[24,8,96]{2,1,0:T(8,128)(2,1)S(1)}, u32[]{:S(2)}, u32[]{:S(2)}) collective-permute-start(bf16[24,8,96]{2,1,0:T(8,128)(2,1)} %get-tuple-element.49), channel_id=1, source_target_pairs={{0,1},{1,0},{2,3},{3,2},{4,5},{5,4},{6,7},{7,6},{8,9},{9,8},{10,11... | collective-permute-start | bytes 110600 | tf_op jit(solution)/shard_map/ppermute | solution.py:657
  19.8 5.6 %collective-permute-start.3 = (bf16[24,8,96]{2,1,0:T(8,128)(2,1)}, bf16[24,8,96]{2,1,0:T(8,128)(2,1)S(1)}, u32[]{:S(2)}, u32[]{:S(2)}) collective-permute-start(bf16[24,8,96]{2,1,0:T(8,128)(2,1)} %get-tuple-element.50), channel_id=1, source_target_pairs={{1,2},{2,1},{3,4},{4,3},{5,6},{6,5},{7,8},{8,7},{9,10},{10,9},{11,... | collective-permute-start | bytes 110600 | tf_op jit(solution)/shard_map/ppermute | solution.py:657
  25.1 0.6 copy-start.4
  25.4 0.6 copy-start.5
  38.0 1.8 %collective-permute-start.4 = (bf16[1024,128]{1,0:T(8,128)(2,1)}, bf16[1024,128]{1,0:T(8,128)(2,1)S(1)}, u32[]{:S(2)}, u32[]{:S(2)}) collective-permute-start(bf16[1024,128]{1,0:T(8,128)(2,1)} %get-tuple-element.73), channel_id=1, source_target_pairs={{0,1},{1,0},{2,3},{3,2},{4,5},{5,4},{6,7},{7,6},{8,9},{9,8},{10,11... | collective-permute-start | bytes 786440 | tf_op jit(solution)/shard_map/ppermute | solution.py:726
  94.7 4.7 %copy-start = (bf16[128,8,128]{2,1,0:T(8,128)(2,1)}, bf16[128,8,128]{2,1,0:T(8,128)(2,1)S(1)}, u32[]{:S(2)}) copy-start(bf16[128,8,128]{2,1,0:T(8,128)(2,1)S(1)} %all_to_all.11) | copy-start | bytes 786436
  94.7 4.7 %collective-permute-start.5 = (bf16[1024,128]{1,0:T(8,128)(2,1)S(1)}, bf16[1024,128]{1,0:T(8,128)(2,1)S(1)}, u32[]{:S(2)}, u32[]{:S(2)}) collective-permute-start(bf16[1024,128]{1,0:T(8,128)(2,1)S(1)} %bitcast.7), channel_id=1, source_target_pairs={{0,1},{1,0},{2,3},{3,2},{4,5},{5,4},{6,7},{7,6},{8,9},{9,8},{10,11... | collective-permute-start | bytes 786440 | tf_op jit(solution)/shard_map/ppermute | solution.py:733
  99.4 0.7 copy-start.3

commit v3 on v2

--- a/solution.py
+++ b/solution.py
@@ -30,7 +30,7 @@
 OWN_PAIRS = 6
 UPPER_PAIRS = 11
 CHUNK = 2
-LIMIT = 60 * 1024 * 1024
+FEED = 256
 
 
 def dot(a, b):
@@ -126,13 +126,8 @@
     return [v[:, p : p + step] for p in range(0, v.shape[1], step)]
 
 
-def across(ref, start, count):
-    return jnp.concatenate([ref[start + p] for p in range(count)], 1)
-
-
-def keep_pairs(ref, start, v):
-    for p, part in enumerate(per_pair(v)):
-        ref[start + p] = part
+def split_lanes(v):
+    return [v[:, p : p + FEED] for p in range(0, v.shape[1], FEED)]
 
 
 def scaled(v, gain):
@@ -174,9 +169,13 @@
     return jnp.concatenate([tokens[:64], tokens[64:]], 1)
 
 
-def head_diagonal(v):
+def by_head(rows, blocks, product):
     return jnp.concatenate(
-        [v[h * HEAD : (h + 1) * HEAD, h * PAIR : (h + 1) * PAIR] for h in range(HEADS)], 0
+        [
+            product(rows[h * HEAD : (h + 1) * HEAD], blocks[:, h * PAIR : (h + 1) * PAIR])
+            for h in range(HEADS)
+        ],
+        0,
     )
 
 
@@ -212,7 +211,7 @@
     probs = jnp.concatenate(probs, 1)
     keep(4, probs)
     mixed = [
-        head_diagonal(dot(part[2 * C :], window_rows(prob)))
+        by_head(part[2 * C :], window_rows(prob), dot)
         for part, prob in zip(parts, per_heads(probs))
     ]
     mix = jnp.concatenate(mixed, 1).astype(BF16)
@@ -223,9 +222,12 @@
     keep(7, r2)
     f = with_ones(scaled(xhat2, w.gain[b, 1]).astype(BF16))
     keep(8, f)
-    u = dot(w.up_t[b], f)
-    m, slope = gelu_parts(u)
-    m = m.astype(BF16)
+    m, slope = [], []
+    for part in split_lanes(f):
+        one, two = gelu_parts(dot(w.up_t[b], part))
+        m.append(one.astype(BF16))
+        slope.append(two.astype(BF16))
+    m, slope = jnp.concatenate(m, 1), jnp.concatenate(slope, 1)
     keep(9, m)
     keep(10, slope)
     out = h + dot(w.down_t[b], m)
@@ -242,19 +244,22 @@
         return sum(per_pair(v))
 
     g16 = g.astype(BF16)
-    du = (dot(w.down[b], g16) * slope).astype(BF16)
-    w.d_down[b] += dot_nt(own(g16), m)
-    w.d_up[b] += dot_nt(own(f), du)
+    du = []
+    for part, part_slope in zip(split_lanes(g16), split_lanes(slope)):
+        du.append((dot(w.down[b], part) * part_slope.astype(F32)).astype(BF16))
+    du = jnp.concatenate(du, 1)
+    w.d_down[b] = dot_nt(own(g16), m)
+    w.d_up[b] = dot_nt(own(f), du)
     df = dot(w.up[b], du)
-    w.d_gain[b, 1] += pairs_sum(own(df * xhat2))
+    w.d_gain[b, 1] = pairs_sum(own(df * xhat2))
     dh = g + norm_back(scaled(df, w.gain[b, 1]), xhat2, r2)
     dh16 = dh.astype(BF16)
-    w.d_proj[b] += dot_nt(mix, own(dh16))
+    w.d_proj[b] = dot_nt(mix, own(dh16))
     dmix = dot(w.proj[b], dh16).astype(BF16)
     parts, d_parts = per_pair(qkv), per_pair(dmix)
     dprobs = [dot(deep_tokens(v[2 * C :]), deep_rows(d)) for v, d in zip(parts, d_parts)]
     ds16 = []
-    d_bias = jnp.zeros((64, HEADS * PAIR), F32)
+    d_bias = None
     for p in range(0, len(parts), CHUNK):
         some = range(p, min(p + CHUNK, len(parts)))
         prob = probs[:, HEADS * PAIR * p : HEADS * PAIR * (p + len(some))].astype(F32)
@@ -264,19 +269,19 @@
         for q, part in zip(some, per_heads(ds)):
             if mask is not None:
                 part = part * jnp.concatenate([per_pair(mask)[q]] * HEADS, 1)
-            d_bias = d_bias + part
-    w.d_bias[b] += d_bias
+            d_bias = part if d_bias is None else d_bias + part
+    w.d_bias[b] = d_bias
     dq, dk, dv = [], [], []
     ds16 = jnp.concatenate(ds16, 1)
     for part, d_part, prob, ds in zip(parts, d_parts, per_heads(probs), per_heads(ds16)):
         ds = window_rows(ds)
-        dv.append(dot_nt(head_blocks(d_part), window_rows(prob)))
-        dk.append(dot_nt(head_blocks(part[:C]), ds) * SCALE)
-        dq.append(head_diagonal(dot(part[C : 2 * C], ds)) * SCALE)
+        dv.append(by_head(d_part, window_rows(prob), dot_nt))
+        dk.append(by_head(part[:C], ds, dot_nt) * SCALE)
+        dq.append(by_head(part[C : 2 * C], ds, dot) * SCALE)
     dqkv = jnp.concatenate([jnp.concatenate(v, 1) for v in (dq, dk, dv)], 0).astype(BF16)
-    w.d_qkv[b] += dot_nt(own(a), dqkv)
+    w.d_qkv[b] = dot_nt(own(a), dqkv)
     da = dot(w.qkv[b], dqkv)
-    w.d_gain[b, 0] += pairs_sum(own(da * xhat1))
+    w.d_gain[b, 0] = pairs_sum(own(da * xhat1))
     return dh + norm_back(scaled(da, w.gain[b, 0]), xhat1, r1)
 
 
@@ -475,8 +480,7 @@
 
 
 def strip_kernel(*refs):
-    sources, (far_a, far_b, sems, send_a, send_b), places = refs[:4], refs[4:9], refs[9:]
-    finish(fetch(zip(sources, places), sems))
+    places, (send_a, send_b) = refs[:4], refs[4:]
     row = lax.axis_index("row")
     both = []
     for cols in (slice(0, 8), slice(TW - 8, TW)):
@@ -491,7 +495,6 @@
     near_part, far_part = to_sides(lax.axis_index(COL_AXES), *both)
     send_a[...] = near_part
     send_b[...] = far_part
-    finish(fetch([(send_a, far_a), (send_b, far_b)], sems))
 
 
 UPPER_IN = [TILE, TILE] + [((8, TW, C), BF16)] * 2 + [((24, 8, C), BF16)] * 2
@@ -520,8 +523,7 @@
     first_row, last_row = row == 0, row == rows_cols[0] - 1
     first_col, last_col = col == 0, col == rows_cols[1] - 1
 
-    for ref in (d_gain, d_qkv, d_proj, d_up, d_down, d_bias, misc):
-        ref[...] = jnp.zeros(ref.shape, F32)
+    misc[...] = jnp.zeros(misc.shape, F32)
     table[...] = jnp.zeros(table.shape, F32)
     finish(copies[:6])
     left, right = sides(col, got_col[0][...].astype(F32), got_col[1][...].astype(F32))
@@ -618,9 +620,8 @@
 
 
 def unpack_kernel(
-    mine_far, other_far, gains, qkv, qkv_bias, table, proj, up, up_bias, down_t, sems, mine, other
+    mine, other, gains, qkv, qkv_bias, table, proj, up, up_bias, down_t
 ):
-    finish(fetch([(mine_far, mine), (other_far, other)], sems))
     core = lax.axis_index("core")
     for b in range(2):
         flat = jnp.where(core == b, mine[...], other[...]).astype(F32)
@@ -657,18 +658,17 @@
     return lax.ppermute(pair[0], axes, near(count)), lax.ppermute(pair[1], axes, far(count))
 
 
-def body(region, cotangent, gains, qkv, qkv_bias, table, proj, up, up_bias, down):
-    rows, cols = lax.axis_size("row"), lax.axis_size(COL_AXES)
-    table_t = jnp.transpose(table, (1, 0, 2))
-    down_t = jnp.transpose(down, (0, 2, 1))
-    params = (gains, qkv_bias, table_t, up_bias, qkv, proj, up, down_t)
-    limit = pltpu.CompilerParams(vmem_limit_bytes=LIMIT)
-
-    def dma(count):
-        return [pltpu.SemaphoreType.DMA((count,))]
-
+def limited(size):
+    return pltpu.CompilerParams(vmem_limit_bytes=size * 1024 * 1024)
+
+
+def dma(count):
+    return [pltpu.SemaphoreType.DMA((count,))]
+
+
+def run_lower(*args):
     strip = ((8, TW, C), BF16)
-    low, send_a, send_b, *saved = pl.pallas_call(
+    return pl.pallas_call(
         lower_kernel,
         out_shape=shapes([TILE, strip, strip] + SAVES),
         in_specs=[HBM] * 10,
@@ -676,31 +676,15 @@
         scratch_shapes=dma(13 + len(SAVES))
         + scratch([((TH, TW, C), F32), TABLE, GAIN, BIAS, TILE, TILE, TILE, strip, strip])
         + scratch(SMALL + FIRST + SAVES),
-        compiler_params=limit,
+        compiler_params=limited(60),
         name="lower",
-    )(region, cotangent, *params)
-    row_got = swap((send_a, send_b), "row", rows)
-    prepared = pl.pallas_call(
-        prepare_kernel,
-        out_shape=shapes(PREPARED),
-        in_specs=[HBM] * 9,
-        out_specs=[HBM] * len(PREPARED),
-        scratch_shapes=dma(8) + scratch([TABLE] + WEIGHTS + SMALL + PREPARED),
-        compiler_params=limit,
-        cost_estimate=pl.CostEstimate(flops=10**9, bytes_accessed=4 * 10**6, transcendentals=0),
-        name="prepare",
-    )(saved[1], *params)
-    strip = ((24, 8, C), BF16)
-    send = pl.pallas_call(
-        strip_kernel,
-        out_shape=shapes([strip, strip]),
-        in_specs=[HBM] * 4,
-        out_specs=[HBM] * 2,
-        scratch_shapes=dma(4) + scratch([strip, strip] + UPPER_IN[:4]),
-        compiler_params=limit,
-        name="strips",
-    )(low, cotangent, *row_got)
-    col_got = swap(send, COL_AXES, cols)
+    )(*args)
+
+
+FLAT = ((ROWS, PAIR), BF16)
+
+
+def run_upper(rows, cols, *args):
     wide = ((TH + 8, TW + 16, C), F32)
     narrow = ((TH + 8, TW + 8, C), F32)
     sums = [
@@ -712,17 +696,48 @@
         ((2, 64, HEADS * PAIR), F32),
     ]
     results = [TILE, ((TH, TW, C), F32)]
-    flat = ((ROWS, PAIR), BF16)
-    out, grad_region, keep, give = pl.pallas_call(
+    return pl.pallas_call(
         functools.partial(upper_kernel, (rows, cols)),
-        out_shape=shapes(results + [flat, flat]),
+        out_shape=shapes(results + [FLAT, FLAT]),
         in_specs=[HBM] * len(UPPER_IN),
         out_specs=[HBM] * 4,
         scratch_shapes=dma(len(UPPER_IN))
         + scratch(results + [((2, ROWS, PAIR), BF16)] + UPPER_IN + [wide, wide, narrow, narrow, TABLE, ((2, 32, PAIR), F32)] + sums),
-        compiler_params=limit,
+        compiler_params=limited(60),
         name="upper",
-    )(low, cotangent, *row_got, *col_got, qkv, proj, up, down_t, *prepared, *saved)
+    )(*args)
+
+
+def body(region, cotangent, gains, qkv, qkv_bias, table, proj, up, up_bias, down):
+    rows, cols = lax.axis_size("row"), lax.axis_size(COL_AXES)
+    table_t = jnp.transpose(table, (1, 0, 2))
+    down_t = jnp.transpose(down, (0, 2, 1))
+    params = (gains, qkv_bias, table_t, up_bias, qkv, proj, up, down_t)
+    low, send_a, send_b, *saved = run_lower(region, cotangent, *params)
+    row_got = swap((send_a, send_b), "row", rows)
+    prepared = pl.pallas_call(
+        prepare_kernel,
+        out_shape=shapes(PREPARED),
+        in_specs=[HBM] * 9,
+        out_specs=[HBM] * len(PREPARED),
+        scratch_shapes=dma(8) + scratch([TABLE] + WEIGHTS + SMALL + PREPARED),
+        compiler_params=limited(60),
+        cost_estimate=pl.CostEstimate(flops=10**9, bytes_accessed=4 * 10**6, transcendentals=0),
+        name="prepare",
+    )(saved[1], *params)
+    strip = ((24, 8, C), BF16)
+    send = pl.pallas_call(
+        strip_kernel,
+        out_shape=shapes([strip, strip]),
+        in_specs=[VMEM] * 4,
+        out_specs=[VMEM] * 2,
+        compiler_params=limited(8),
+        name="strips",
+    )(low, cotangent, *row_got)
+    col_got = swap(send, COL_AXES, cols)
+    out, grad_region, keep, give = run_upper(
+        rows, cols, low, cotangent, *row_got, *col_got, qkv, proj, up, down_t, *prepared, *saved
+    )
     got = lax.ppermute(give, "core", near(2))
     share = (keep.astype(F32) + got.astype(F32)).astype(BF16).reshape(PEERS, -1, PAIR)
     peers = ("row", "col_half")
@@ -746,10 +761,9 @@
                 (2, C, HID),
             )
         ),
-        in_specs=[HBM] * 2,
+        in_specs=[VMEM] * 2,
         out_specs=[VMEM] * 8,
-        scratch_shapes=dma(2) + scratch([flat, flat]),
-        compiler_params=limit,
+        compiler_params=limited(8),
         name="unpack",
     )(mine, other)
     d_gains, d_qkv, d_qkv_bias, d_table, d_proj, d_up, d_up_bias, d_down_t = grads

time: 103 us -> 99.5 us (0.966)
  Pallas kernels: 22.6 us -> 20.1 us
    pallas_call x1, Pallas kernels: 1.84 us -> 0.05 us  [body(): pl.pallas_call(strip_kernel, out_shape=shapes([strip, strip]), in_specs=[...]
    pallas_call x1, Pallas kernels: 2.04 us -> 1 us  [body(): pl.pallas_call(unpack_kernel, out_shape=tuple((jax.ShapeDtypeStruct(shape...]
  transfers between devices with their start and end apart: 6 -> 6, of which waited for: 4 -> 3; matrix products, arithmetic and copies ran while one was open for 0% -> 0% of each run, Pallas kernels for 2% -> 2%
where the time goes in v3:
time: 99.5 us; the launch traced here: 99.2 us
  blocking collectives  53.7 us (54%)
  Pallas kernels  20.1 us (20%)
  starting transfers between devices  17.2 us (17%)
  waiting for transfers between devices  4.59 us (5%)
  local copies, waits for them, and re-layouts  1.67 us (2%)
  other arithmetic  1.16 us (1%)
    all_to_all x1, blocking collectives, body(): parts = lax.all_to_all(share, peers, 0, 0)  35.2 us
    all_to_all x1, blocking collectives, body(): mine = lax.all_to_all(jnp.broadcast_to(part, share.shape), peers, 0, 0)  18.5 us
    pallas_call x1, Pallas kernels, run_upper(): pl.pallas_call(functools.partial(upper_kernel, (rows, cols)), out_shape=s...  12.3 us
    ppermute x2, starting transfers between devices, swap(): lax.ppermute(pair[0], axes, near(count))  9.83 us
    pallas_call x1, Pallas kernels, run_lower(): pl.pallas_call(lower_kernel, out_shape=shapes([TILE, strip, strip] + SAVE...  4.48 us
    ppermute x2, starting transfers between devices, swap(): lax.ppermute(pair[1], axes, far(count))  3.67 us
    ppermute x1, starting transfers between devices, body(): other = lax.ppermute(mine, 'core', near(2))  3.56 us
    pallas_call x1, Pallas kernels, body(): pl.pallas_call(prepare_kernel, out_shape=shapes(PREPARED), in_specs=[HBM]...  2.31 us
  transfers between devices with their start and end apart: 6, of which 3 were waited for; matrix products, arithmetic and copies ran while one was open for 0% of the time, Pallas kernels for 2%

profile of v3, /device:TPU:1, one launch (start us, length us, event | category | flops | bytes accessed | tf_op | source)
XLA Modules:
  0.0 99.2 jit_solution(2306970832298982858)
XLA Ops:
  0.6 0.0 copy-start
  0.7 4.5 %lower.1 = (bf16[16,48,96]{2,1,0:T(8,128)(2,1)}, bf16[8,48,96]{2,1,0:T(8,128)(2,1)}, bf16[8,48,96]{2,1,0:T(8,128)(2,1)}, f32[6,96,128]{2,1,0:T(8,128)}, f32[6,1,...) custom-call(bf16[16,48,96]{2,1,0:T(8,128)(2,1)} %region.1, ...), custom_call_target="tpu_custom_call" | custom-call | tf_op jit(solution)/shard_map/lower/pallas_call | solution.py:671
  5.1 7.8 %collective-permute-start = (bf16[8,48,96]{2,1,0:T(8,128)(2,1)}, bf16[8,48,96]{2,1,0:T(8,128)(2,1)S(1)}, u32[]{:S(2)}, u32[]{:S(2)}) collective-permute-start(bf16[8,48,96]{2,1,0:T(8,128)(2,1)} %get-tuple-element.47), channel_id=1, source_target_pairs={{0,32},{32,0},{64,96},{96,64},{128,160},{160,128},{192,224},{224,1... | collective-permute-start | bytes 221192 | tf_op jit(solution)/shard_map/ppermute | solution.py:658
  13.0 0.7 collective-permute-start.1
  13.6 1.7 %collective-permute-done.refs_2_.rest_2_ = bf16[8,48,96]{2,1,0:T(8,128)(2,1)S(1)} collective-permute-done((bf16[8,48,96]{2,1,0:T(8,128)(2,1)}, bf16[8,48,96]{2,1,0:T(8,128)(2,1)S(1)}, u32[]{:S(2)}, u32[]{:S(2)}) %collective-permute-start) | collective-permute-done | bytes 73760 | tf_op jit(solution)/shard_map/ppermute | solution.py:658
  15.3 0.0 collective-permute-done.1.refs_3_.rest_3_
  15.3 1.0 copy-done.1
  16.3 0.1 strips.1
  16.4 2.0 %collective-permute-start.2 = (bf16[24,8,96]{2,1,0:T(8,128)(2,1)S(1)}, bf16[24,8,96]{2,1,0:T(8,128)(2,1)S(1)}, u32[]{:S(2)}, u32[]{:S(2)}) collective-permute-start(bf16[24,8,96]{2,1,0:T(8,128)(2,1)S(1)} %get-tuple-element.49), channel_id=1, source_target_pairs={{0,1},{1,0},{2,3},{3,2},{4,5},{5,4},{6,7},{7,6},{8,9},{9,8},{10,11... | collective-permute-start | bytes 110600 | tf_op jit(solution)/shard_map/ppermute | solution.py:658
  18.4 3.0 %collective-permute-start.3 = (bf16[24,8,96]{2,1,0:T(8,128)(2,1)S(1)}, bf16[24,8,96]{2,1,0:T(8,128)(2,1)S(1)}, u32[]{:S(2)}, u32[]{:S(2)}) collective-permute-start(bf16[24,8,96]{2,1,0:T(8,128)(2,1)S(1)} %get-tuple-element.50), channel_id=1, source_target_pairs={{1,2},{2,1},{3,4},{4,3},{5,6},{6,5},{7,8},{8,7},{9,10},{10,9},{11,... | collective-permute-start | bytes 110600 | tf_op jit(solution)/shard_map/ppermute | solution.py:658
  21.4 2.3 %prepare.1 = (f32[2,96,128]{2,1,0:T(8,128)}, f32[2,96,128]{2,1,0:T(8,128)}, f32[64,384]{1,0:T(8,128)}, bf16[288,112]{1,0:T(8,128)(2,1)}, bf16[96,96]{1,0:T(8,128...) custom-call(f32[6,1,128]{2,1,0:T(1,128)} %get-tuple-element.51.after.rest_19_, ...), custom_call_target="tpu_custom_call" | custom-call | flops 1000000000 | bytes 4000000 | tf_op jit(solution)/shard_map/prepare/pallas_call | solution.py:718
  23.7 0.0 collective-permute-done.3.rest_5_
  23.8 0.6 copy-done.4
  24.4 0.1 copy-done.5
  24.4 12.3 %upper.1 = (bf16[16,48,96]{2,1,0:T(8,128)(2,1)}, f32[16,48,96]{2,1,0:T(8,128)}, bf16[1024,128]{1,0:T(8,128)(2,1)}, bf16[1024,128]{1,0:T(8,128)(2,1)}) custom-call(bf16[16,48,96]{2,1,0:T(8,128)(2,1)} %get-tuple-element.46.refs_0_.rest_0_, bf16[16,48,96]{2,1,0:T(8,128)(2,1)} %rest_1_.1, bf16[8,48,96]{2,1,0:T(8,128)(2,1)} %copy-done.2, ...), custom_call_target="tpu_custom_call" | custom-call | tf_op jit(solution)/shard_map/upper/pallas_call | solution.py:699
  36.7 0.1 collective-permute-start.4
  36.8 1.7 %collective-permute-done.4 = bf16[1024,128]{1,0:T(8,128)(2,1)S(1)} collective-permute-done((bf16[1024,128]{1,0:T(8,128)(2,1)}, bf16[1024,128]{1,0:T(8,128)(2,1)S(1)}, u32[]{:S(2)}, u32[]{:S(2)}) %collective-permute-start.4) | collective-permute-done | bytes 262176 | tf_op jit(solution)/shard_map/ppermute | solution.py:741
  38.5 1.0 %fusion = bf16[128,8,128]{2,1,0:T(8,128)(2,1)S(1)} fusion(bf16[1024,128]{1,0:T(8,128)(2,1)S(1)} %collective-permute-done.4, bf16[1024,128]{1,0:T(8,128)(2,1)} %get-tuple-element.72), kind=kLoop, calls=%fused_computation.1 | loop fusion | flops 524288 | bytes 786432 | tf_op jit(solution)/shard_map/reshape | solution.py:742
  39.6 35.2 %all_to_all.10 = bf16[128,8,128]{2,1,0:T(8,128)(2,1)S(1)} all-to-all(bf16[128,8,128]{2,1,0:T(8,128)(2,1)S(1)} %fusion), channel_id=1, replica_groups=mesh['row'=8,'col_half'=16,'core'=2] {'row','col_half'}, dimensions={0} | all-to-all | bytes 524288 | tf_op jit(solution)/shard_map/all_to_all | solution.py:744
  74.7 0.1 reduce_sum.12
  74.9 18.5 %all_to_all.11 = bf16[128,8,128]{2,1,0:T(8,128)(2,1)S(1)} all-to-all(bf16[128,8,128]{2,1,0:T(8,128)(2,1)S(1)} %broadcast_in_dim.2), channel_id=1, replica_groups=mesh['row'=8,'col_half'=16,'core'=2] {'row','col_half'}, dimensions={0} | all-to-all | bytes 524288 | tf_op jit(solution)/shard_map/all_to_all | solution.py:746
  93.4 3.6 %collective-permute-start.5 = (bf16[1024,128]{1,0:T(8,128)(2,1)S(1)}, bf16[1024,128]{1,0:T(8,128)(2,1)S(1)}, u32[]{:S(2)}, u32[]{:S(2)}) collective-permute-start(bf16[1024,128]{1,0:T(8,128)(2,1)S(1)} %bitcast.7), channel_id=1, source_target_pairs={{0,1},{1,0},{2,3},{3,2},{4,5},{5,4},{6,7},{7,6},{8,9},{9,8},{10,11... | collective-permute-start | bytes 786440 | tf_op jit(solution)/shard_map/ppermute | solution.py:748
  97.0 1.2 %collective-permute-done.5.other = bf16[1024,128]{1,0:T(8,128)(2,1)S(1)} collective-permute-done((bf16[1024,128]{1,0:T(8,128)(2,1)S(1)}, bf16[1024,128]{1,0:T(8,128)(2,1)S(1)}, u32[]{:S(2)}, u32[]{:S(2)}) %collective-permute-start.5) | collective-permute-done | bytes 262176 | tf_op jit(solution)/shard_map/ppermute | solution.py:748
  98.2 1.0 %unpack.1 = (f32[2,2,96]{2,1,0:T(2,128)}, f32[2,96,288]{2,1,0:T(8,128)}, f32[2,288]{1,0:T(2,128)}, f32[3,2,225]{2,1,0:T(2,128)}, f32[2,96,96]{2,1,0:T(8,128)}, /...) custom-call(bf16[1024,128]{1,0:T(8,128)(2,1)S(1)} %bitcast.8, ...), custom_call_target="tpu_custom_call" | custom-call | tf_op jit(solution)/shard_map/unpack/pallas_call | solution.py:749
  (10 shorter events, 0.1 us)
Async XLA Ops:
  0.6 14.7 %copy-start = (bf16[16,48,96]{2,1,0:T(8,128)(2,1)S(1)}, bf16[16,48,96]{2,1,0:T(8,128)(2,1)}, u32[]{:S(2)}) copy-start(bf16[16,48,96]{2,1,0:T(8,128)(2,1)} %rest_1_.1) | copy-start | bytes 442372
  5.1 10.1 %collective-permute-start = (bf16[8,48,96]{2,1,0:T(8,128)(2,1)}, bf16[8,48,96]{2,1,0:T(8,128)(2,1)S(1)}, u32[]{:S(2)}, u32[]{:S(2)}) collective-permute-start(bf16[8,48,96]{2,1,0:T(8,128)(2,1)} %get-tuple-element.47), channel_id=1, source_target_pairs={{0,32},{32,0},{64,96},{96,64},{128,160},{160,128},{192,224},{224,1... | collective-permute-start | bytes 221192 | tf_op jit(solution)/shard_map/ppermute | solution.py:658
  13.0 2.3 %collective-permute-start.1 = (bf16[8,48,96]{2,1,0:T(8,128)(2,1)}, bf16[8,48,96]{2,1,0:T(8,128)(2,1)S(1)}, u32[]{:S(2)}, u32[]{:S(2)}) collective-permute-start(bf16[8,48,96]{2,1,0:T(8,128)(2,1)} %get-tuple-element.48), channel_id=1, source_target_pairs={{32,64},{64,32},{96,128},{128,96},{160,192},{192,160},{33,65},{65,... | collective-permute-start | bytes 221192 | tf_op jit(solution)/shard_map/ppermute | solution.py:658
  15.3 1.1 %copy-start.2 = (bf16[8,48,96]{2,1,0:T(8,128)(2,1)}, bf16[8,48,96]{2,1,0:T(8,128)(2,1)S(1)}, u32[]{:S(2)}) copy-start(bf16[8,48,96]{2,1,0:T(8,128)(2,1)S(1)} %collective-permute-done.refs_2_.rest_2_) | copy-start | bytes 221188
  15.3 1.1 %copy-start.3 = (bf16[8,48,96]{2,1,0:T(8,128)(2,1)}, bf16[8,48,96]{2,1,0:T(8,128)(2,1)S(1)}, u32[]{:S(2)}) copy-start(bf16[8,48,96]{2,1,0:T(8,128)(2,1)S(1)} %collective-permute-done.1.refs_3_.rest_3_) | copy-start | bytes 221188
  15.3 1.0 %copy-start.1 = (bf16[16,48,96]{2,1,0:T(8,128)(2,1)S(1)}, bf16[16,48,96]{2,1,0:T(8,128)(2,1)}, u32[]{:S(2)}) copy-start(bf16[16,48,96]{2,1,0:T(8,128)(2,1)} %get-tuple-element.46.refs_0_.rest_0_) | copy-start | bytes 442372
  16.4 7.4 %collective-permute-start.2 = (bf16[24,8,96]{2,1,0:T(8,128)(2,1)S(1)}, bf16[24,8,96]{2,1,0:T(8,128)(2,1)S(1)}, u32[]{:S(2)}, u32[]{:S(2)}) collective-permute-start(bf16[24,8,96]{2,1,0:T(8,128)(2,1)S(1)} %get-tuple-element.49), channel_id=1, source_target_pairs={{0,1},{1,0},{2,3},{3,2},{4,5},{5,4},{6,7},{7,6},{8,9},{9,8},{10,11... | collective-permute-start | bytes 110600 | tf_op jit(solution)/shard_map/ppermute | solution.py:658
  18.4 5.4 %collective-permute-start.3 = (bf16[24,8,96]{2,1,0:T(8,128)(2,1)S(1)}, bf16[24,8,96]{2,1,0:T(8,128)(2,1)S(1)}, u32[]{:S(2)}, u32[]{:S(2)}) collective-permute-start(bf16[24,8,96]{2,1,0:T(8,128)(2,1)S(1)} %get-tuple-element.50), channel_id=1, source_target_pairs={{1,2},{2,1},{3,4},{4,3},{5,6},{6,5},{7,8},{8,7},{9,10},{10,9},{11,... | collective-permute-start | bytes 110600 | tf_op jit(solution)/shard_map/ppermute | solution.py:658
  23.7 0.6 copy-start.4
  23.8 0.6 copy-start.5
  36.7 1.8 %collective-permute-start.4 = (bf16[1024,128]{1,0:T(8,128)(2,1)}, bf16[1024,128]{1,0:T(8,128)(2,1)S(1)}, u32[]{:S(2)}, u32[]{:S(2)}) collective-permute-start(bf16[1024,128]{1,0:T(8,128)(2,1)} %get-tuple-element.73), channel_id=1, source_target_pairs={{0,1},{1,0},{2,3},{3,2},{4,5},{5,4},{6,7},{7,6},{8,9},{9,8},{10,11... | collective-permute-start | bytes 786440 | tf_op jit(solution)/shard_map/ppermute | solution.py:741
  93.4 4.7 %collective-permute-start.5 = (bf16[1024,128]{1,0:T(8,128)(2,1)S(1)}, bf16[1024,128]{1,0:T(8,128)(2,1)S(1)}, u32[]{:S(2)}, u32[]{:S(2)}) collective-permute-start(bf16[1024,128]{1,0:T(8,128)(2,1)S(1)} %bitcast.7), channel_id=1, source_target_pairs={{0,1},{1,0},{2,3},{3,2},{4,5},{5,4},{6,7},{7,6},{8,9},{9,8},{10,11... | collective-permute-start | bytes 786440 | tf_op jit(solution)/shard_map/ppermute | solution.py:748

commit v4 on v3

--- a/solution.py
+++ b/solution.py
@@ -30,6 +30,7 @@
 OWN_PAIRS = 6
 UPPER_PAIRS = 11
 CHUNK = 2
+EARLY = 9
 FEED = 256
 
 
@@ -405,7 +406,7 @@
     far_b,
     *rest,
 ):
-    saves, rest = rest[: len(SAVES)], rest[len(SAVES) :]
+    saves, rest = rest[:EARLY], rest[EARLY:]
     sems, field, table, gain, bias, tile, cot_tile, low, send_a, send_b, *rest = rest
     small, weights, kept = rest[:4], rest[4:8], rest[8:]
     sources = [norm_gains, qkv_bias, bias_table, up_bias]
@@ -425,6 +426,8 @@
     leaving = []
 
     def keep(k, value):
+        if k >= EARLY:
+            return
         ref = kept[k]
         parts = per_heads(value) if ref.shape[2] == HEADS * PAIR else per_pair(value)
         for n, part in enumerate(parts):
@@ -447,7 +450,7 @@
 
 
 def prepare_kernel(
-    after,
+    feed,
     norm_gains,
     qkv_bias,
     bias_table,
@@ -458,13 +461,19 @@
     down_t,
     *rest,
 ):
-    far, (sems, table), rest = rest[:8], rest[8:10], rest[10:]
+    far, (sems, table, f), rest = rest[:10], rest[10:13], rest[13:]
     (qkv, proj, up, down_copy), small, made = rest[:4], rest[4:8], rest[8:]
-    gain_0, gain_1, bias, qkv_t, proj_t, up_t, down_0, down_1 = made
+    gain_0, gain_1, bias, qkv_t, proj_t, up_t, down_0, down_1, m, slope = made
     sources = [norm_gains, qkv_bias, bias_table, up_bias]
     sources += [qkv_weight, proj_weight, up_weight, down_t]
-    finish(fetch(zip(sources, list(small) + [qkv, proj, up, down_copy]), sems))
+    finish(fetch(zip([feed] + sources, [f, *small, qkv, proj, up, down_copy]), sems))
     norm_gains, qkv_bias, bias_table, up_bias = small
+    lower_up_t = augmented(up[0], up_bias[0:1, :])
+    for n in range(OWN_PAIRS):
+        one, two = gelu_parts(dot(lower_up_t, f[n]))
+        m[n] = one.astype(BF16)
+        slope[n] = two.astype(BF16)
+    leaving = fetch([(m, far[8]), (slope, far[9])], sems.at[pl.ds(8, 2)])
     for b, gain in enumerate((gain_0, gain_1)):
         gain[0], gain[1] = wide_gains(norm_gains, b)
     keep_bias(bias, table, bias_table, 1)
@@ -473,21 +482,29 @@
     up_t[...] = augmented(up[1], up_bias[1:2, :])
     down_0[...] = transposed(down_copy[0])
     down_1[...] = transposed(down_copy[1])
-    finish(fetch(zip(made, far), sems))
+    finish(leaving + fetch(zip(made[:8], far), sems))
 
 
 PREPARED = [GAIN, GAIN, BIAS, QKV_T, PROJ_T, UP_T, DOWN, DOWN]
 
 
-def strip_kernel(*refs):
-    places, (send_a, send_b) = refs[:4], refs[4:]
+SIDE_COLUMNS = (slice(0, 8), slice(TW - 8, TW))
+
+
+def own_kernel(low, cot, own):
+    for side, cols in enumerate(SIDE_COLUMNS):
+        own[side, 0] = low[:, cols]
+        own[side, 1] = cot[:, cols]
+
+
+def strip_kernel(own, row_a, row_b, send_a, send_b):
     row = lax.axis_index("row")
     both = []
-    for cols in (slice(0, 8), slice(TW - 8, TW)):
+    for side, cols in enumerate(SIDE_COLUMNS):
         strips = []
-        for n, own in enumerate(places[:2]):
-            above, below = sides(row, places[2][4 * n : 4 * n + 4], places[3][4 * n : 4 * n + 4])
-            tall = [v.astype(F32) for v in (above[:, cols], own[:, cols], below[:, cols])]
+        for n in range(2):
+            above, below = sides(row, row_a[4 * n : 4 * n + 4], row_b[4 * n : 4 * n + 4])
+            tall = [v.astype(F32) for v in (above[:, cols], own[side, n], below[:, cols])]
             tall = jnp.concatenate(tall, 0)
             half = tall[:, 0:4] if cols.start == 0 else tall[:, 4:8]
             strips.append(jnp.concatenate([half[0:12], half[12:24]], 1))
@@ -585,13 +602,7 @@
 
     g = jnp.concatenate([windows_t(grad_field, p, 4, 4) for p in places[:OWN_PAIRS]], 1)
     finish(copies[18:])
-    saved = [jnp.concatenate([ref[n] for n in range(OWN_PAIRS)], 1) for ref in saves]
-    dx = backward(g, 0, w, saved, None)
-    for p, part in zip(places, per_pair(dx)):
-        windows_back(part, grad_region, p)
-    leaving += fetch([(grad_region, grad_far)], sems.at[pl.ds(1, 1)])
-
-    for b in range(2):
+    def pack(b):
         for j in range(3):
             lanes = slice(j * PAIR, (j + 1) * PAIR)
             packed[b, j * C : (j + 1) * C, :] = d_up[b, 0:C, lanes].astype(BF16)
@@ -614,6 +625,15 @@
         misc[b, 16:24, :] = rows[:, PAIR:]
         packed[b, 864:896, :] = misc[b].astype(BF16)
         packed[b, 896:ROWS, :] = jnp.zeros((ROWS - 896, PAIR), BF16)
+
+    saved = [jnp.concatenate([ref[n] for n in range(OWN_PAIRS)], 1) for ref in saves]
+    dx = backward(g, 0, w, saved, None)
+    for p, part in zip(places, per_pair(dx)):
+        windows_back(part, grad_region, p)
+    leaving += fetch([(grad_region, grad_far)], sems.at[pl.ds(1, 1)])
+
+    pack(0)
+    pack(1)
     core = lax.axis_index("core")
     pairs = [(packed.at[core], keep_far), (packed.at[1 - core], give_far)]
     finish(leaving + fetch(pairs, sems.at[pl.ds(2, 2)]))
@@ -655,7 +675,8 @@
 
 
 def swap(pair, axes, count):
-    return lax.ppermute(pair[0], axes, near(count)), lax.ppermute(pair[1], axes, far(count))
+    second = lax.ppermute(pair[1], axes, far(count))
+    return lax.ppermute(pair[0], axes, near(count)), second
 
 
 def limited(size):
@@ -670,12 +691,12 @@
     strip = ((8, TW, C), BF16)
     return pl.pallas_call(
         lower_kernel,
-        out_shape=shapes([TILE, strip, strip] + SAVES),
+        out_shape=shapes([TILE, strip, strip] + SAVES[:EARLY]),
         in_specs=[HBM] * 10,
-        out_specs=[HBM] * (3 + len(SAVES)),
-        scratch_shapes=dma(13 + len(SAVES))
+        out_specs=[HBM] * (3 + EARLY),
+        scratch_shapes=dma(13 + EARLY)
         + scratch([((TH, TW, C), F32), TABLE, GAIN, BIAS, TILE, TILE, TILE, strip, strip])
-        + scratch(SMALL + FIRST + SAVES),
+        + scratch(SMALL + FIRST + SAVES[:EARLY]),
         compiler_params=limited(60),
         name="lower",
     )(*args)
@@ -715,28 +736,38 @@
     params = (gains, qkv_bias, table_t, up_bias, qkv, proj, up, down_t)
     low, send_a, send_b, *saved = run_lower(region, cotangent, *params)
     row_got = swap((send_a, send_b), "row", rows)
-    prepared = pl.pallas_call(
+    *prepared, m, slope = pl.pallas_call(
         prepare_kernel,
-        out_shape=shapes(PREPARED),
+        out_shape=shapes(PREPARED + SAVES[EARLY:]),
         in_specs=[HBM] * 9,
-        out_specs=[HBM] * len(PREPARED),
-        scratch_shapes=dma(8) + scratch([TABLE] + WEIGHTS + SMALL + PREPARED),
+        out_specs=[HBM] * 10,
+        scratch_shapes=dma(10)
+        + scratch([TABLE, SAVES[8]] + WEIGHTS + SMALL + PREPARED + SAVES[EARLY:]),
         compiler_params=limited(60),
         cost_estimate=pl.CostEstimate(flops=10**9, bytes_accessed=4 * 10**6, transcendentals=0),
         name="prepare",
-    )(saved[1], *params)
+    )(saved[8], *params)
+    own = pl.pallas_call(
+        own_kernel,
+        out_shape=jax.ShapeDtypeStruct((2, 2, TH, 8, C), BF16),
+        in_specs=[VMEM] * 2,
+        out_specs=VMEM,
+        compiler_params=limited(8),
+        cost_estimate=pl.CostEstimate(flops=10**9, bytes_accessed=10**6, transcendentals=0),
+        name="own_strips",
+    )(low, cotangent)
     strip = ((24, 8, C), BF16)
     send = pl.pallas_call(
         strip_kernel,
         out_shape=shapes([strip, strip]),
-        in_specs=[VMEM] * 4,
+        in_specs=[VMEM] * 3,
         out_specs=[VMEM] * 2,
         compiler_params=limited(8),
         name="strips",
-    )(low, cotangent, *row_got)
+    )(own, *row_got)
     col_got = swap(send, COL_AXES, cols)
     out, grad_region, keep, give = run_upper(
-        rows, cols, low, cotangent, *row_got, *col_got, qkv, proj, up, down_t, *prepared, *saved
+        rows, cols, low, cotangent, *row_got, *col_got, qkv, proj, up, down_t, *prepared, *saved, m, slope
     )
     got = lax.ppermute(give, "core", near(2))
     share = (keep.astype(F32) + got.astype(F32)).astype(BF16).reshape(PEERS, -1, PAIR)

time: 99.5 us -> 98.6 us (level)
  blocking collectives: 53.7 us -> 52.6 us
  waiting for transfers between devices: 4.59 us -> 3.59 us
    pallas_call x1 -> x2, Pallas kernels: 2.31 us -> 3.51 us  [the longest x1 3.48 us: body(): pl.pallas_call(prepare_kernel, out_shape=shapes(PREPARED + SAVES[EARLY:])...]
    all_to_all x1, blocking collectives: 35.2 us -> 34.1 us  [body(): parts = lax.all_to_all(share, peers, 0, 0)]
    ppermute x4, waiting for transfers between devices: 1.69 us -> 0.7 us  [the longest x2 0.69 us: swap(): return (lax.ppermute(pair[0], axes, near(count)), second)]
  transfers between devices with their start and end apart: 6 -> 6, of which waited for: 3 -> 3; matrix products, arithmetic and copies ran while one was open for 0% -> 0% of each run, Pallas kernels for 2% -> 4%
where the time goes in v4:
time: 98.6 us; the launch traced here: 98.3 us
  blocking collectives  52.6 us (53%)
  Pallas kernels  20.9 us (21%)
  starting transfers between devices  17.1 us (17%)
  waiting for transfers between devices  3.59 us (4%)
  local copies, waits for them, and re-layouts  2.2 us (2%)
  other arithmetic  1.16 us (1%)
    all_to_all x1, blocking collectives, body(): parts = lax.all_to_all(share, peers, 0, 0)  34.1 us
    all_to_all x1, blocking collectives, body(): mine = lax.all_to_all(jnp.broadcast_to(part, share.shape), peers, 0, 0)  18.5 us
    pallas_call x1, Pallas kernels, run_upper(): pl.pallas_call(functools.partial(upper_kernel, (rows, cols)), out_shape=s...  12.3 us
    ppermute x2, starting transfers between devices, swap(): return (lax.ppermute(pair[0], axes, near(count)), second)  9.75 us
    pallas_call x1, Pallas kernels, run_lower(): pl.pallas_call(lower_kernel, out_shape=shapes([TILE, strip, strip] + SAVE...  4.1 us
    ppermute x2, starting transfers between devices, swap(): second = lax.ppermute(pair[1], axes, far(count))  3.66 us
    ppermute x1, starting transfers between devices, body(): other = lax.ppermute(mine, 'core', near(2))  3.56 us
    pallas_call x1, Pallas kernels, body(): pl.pallas_call(prepare_kernel, out_shape=shapes(PREPARED + SAVES[EARLY:])...  3.48 us
  transfers between devices with their start and end apart: 6, of which 3 were waited for; matrix products, arithmetic and copies ran while one was open for 0% of the time, Pallas kernels for 4%

profile of v4, /device:TPU:1, one launch (start us, length us, event | category | flops | bytes accessed | tf_op | source)
XLA Modules:
  0.0 98.3 jit_solution(2259066629412983672)
XLA Ops:
  0.6 0.0 copy-start
  0.7 4.1 %lower.1 = (bf16[16,48,96]{2,1,0:T(8,128)(2,1)}, bf16[8,48,96]{2,1,0:T(8,128)(2,1)}, bf16[8,48,96]{2,1,0:T(8,128)(2,1)}, f32[6,96,128]{2,1,0:T(8,128)}, f32[6,1,...) custom-call(bf16[16,48,96]{2,1,0:T(8,128)(2,1)} %region.1, ...), custom_call_target="tpu_custom_call" | custom-call | tf_op jit(solution)/shard_map/lower/pallas_call | solution.py:692
  4.8 7.8 %collective-permute-start = (bf16[8,48,96]{2,1,0:T(8,128)(2,1)}, bf16[8,48,96]{2,1,0:T(8,128)(2,1)S(1)}, u32[]{:S(2)}, u32[]{:S(2)}) collective-permute-start(bf16[8,48,96]{2,1,0:T(8,128)(2,1)} %get-tuple-element.47), channel_id=1, source_target_pairs={{0,32},{32,0},{64,96},{96,64},{128,160},{160,128},{192,224},{224,1... | collective-permute-start | bytes 221192 | tf_op jit(solution)/shard_map/ppermute | solution.py:679
  12.6 0.7 collective-permute-start.1
  13.3 0.9 copy-done.3
  14.2 0.7 collective-permute-done.row_a.rest_2_
  14.9 0.1 strips.1
  15.0 0.6 copy-done.1
  15.6 0.0 copy-done.2
  15.6 1.9 %collective-permute-start.2 = (bf16[24,8,96]{2,1,0:T(8,128)(2,1)S(1)}, bf16[24,8,96]{2,1,0:T(8,128)(2,1)S(1)}, u32[]{:S(2)}, u32[]{:S(2)}) collective-permute-start(bf16[24,8,96]{2,1,0:T(8,128)(2,1)S(1)} %get-tuple-element.49), channel_id=1, source_target_pairs={{0,1},{1,0},{2,3},{3,2},{4,5},{5,4},{6,7},{7,6},{8,9},{9,8},{10,11... | collective-permute-start | bytes 110600 | tf_op jit(solution)/shard_map/ppermute | solution.py:679
  17.5 3.0 %collective-permute-start.3 = (bf16[24,8,96]{2,1,0:T(8,128)(2,1)S(1)}, bf16[24,8,96]{2,1,0:T(8,128)(2,1)S(1)}, u32[]{:S(2)}, u32[]{:S(2)}) collective-permute-start(bf16[24,8,96]{2,1,0:T(8,128)(2,1)S(1)} %get-tuple-element.50), channel_id=1, source_target_pairs={{1,2},{2,1},{3,4},{4,3},{5,6},{6,5},{7,8},{8,7},{9,10},{10,9},{11,... | collective-permute-start | bytes 110600 | tf_op jit(solution)/shard_map/ppermute | solution.py:678
  20.5 3.5 %prepare.1 = (f32[2,96,128]{2,1,0:T(8,128)}, f32[2,96,128]{2,1,0:T(8,128)}, f32[64,384]{1,0:T(8,128)}, bf16[288,112]{1,0:T(8,128)(2,1)}, bf16[96,96]{1,0:T(8,128...) custom-call(bf16[6,112,128]{2,1,0:T(8,128)(2,1)} %get-tuple-element., ...), custom_call_target="tpu_custom_call" | custom-call | flops 1000000000 | bytes 4000000 | tf_op jit(solution)/shard_map/prepare/pallas_call | solution.py:739
  24.0 0.6 copy-done.4
  24.6 0.0 copy-done.5
  24.7 12.3 %upper.1 = (bf16[16,48,96]{2,1,0:T(8,128)(2,1)}, f32[16,48,96]{2,1,0:T(8,128)}, bf16[1024,128]{1,0:T(8,128)(2,1)}, bf16[1024,128]{1,0:T(8,128)(2,1)}) custom-call(bf16[16,48,96]{2,1,0:T(8,128)(2,1)} %get-tuple-element.46.low.rest_0_, bf16[16,48,96]{2,1,0:T(8,128)(2,1)} %rest_1_.1, bf16[8,48,96]{2,1,0:T(8,128)(2,1)} %copy-done.1, ...), custom_call_target="tpu_custom_call" | custom-call | tf_op jit(solution)/shard_map/upper/pallas_call | solution.py:720
  37.0 0.1 collective-permute-start.4
  37.1 1.7 %collective-permute-done.4 = bf16[1024,128]{1,0:T(8,128)(2,1)S(1)} collective-permute-done((bf16[1024,128]{1,0:T(8,128)(2,1)}, bf16[1024,128]{1,0:T(8,128)(2,1)S(1)}, u32[]{:S(2)}, u32[]{:S(2)}) %collective-permute-start.4) | collective-permute-done | bytes 262176 | tf_op jit(solution)/shard_map/ppermute | solution.py:772
  38.8 1.0 %fusion = bf16[128,8,128]{2,1,0:T(8,128)(2,1)S(1)} fusion(bf16[1024,128]{1,0:T(8,128)(2,1)S(1)} %collective-permute-done.4, bf16[1024,128]{1,0:T(8,128)(2,1)} %get-tuple-element.72), kind=kLoop, calls=%fused_computation.1 | loop fusion | flops 524288 | bytes 786432 | tf_op jit(solution)/shard_map/reshape | solution.py:773
  39.8 34.1 %all_to_all.10 = bf16[128,8,128]{2,1,0:T(8,128)(2,1)S(1)} all-to-all(bf16[128,8,128]{2,1,0:T(8,128)(2,1)S(1)} %fusion), channel_id=1, replica_groups=mesh['row'=8,'col_half'=16,'core'=2] {'row','col_half'}, dimensions={0} | all-to-all | bytes 524288 | tf_op jit(solution)/shard_map/all_to_all | solution.py:775
  73.9 0.1 reduce_sum.12
  74.1 18.5 %all_to_all.11 = bf16[128,8,128]{2,1,0:T(8,128)(2,1)S(1)} all-to-all(bf16[128,8,128]{2,1,0:T(8,128)(2,1)S(1)} %broadcast_in_dim.2), channel_id=1, replica_groups=mesh['row'=8,'col_half'=16,'core'=2] {'row','col_half'}, dimensions={0} | all-to-all | bytes 524288 | tf_op jit(solution)/shard_map/all_to_all | solution.py:777
  92.6 3.6 %collective-permute-start.5 = (bf16[1024,128]{1,0:T(8,128)(2,1)S(1)}, bf16[1024,128]{1,0:T(8,128)(2,1)S(1)}, u32[]{:S(2)}, u32[]{:S(2)}) collective-permute-start(bf16[1024,128]{1,0:T(8,128)(2,1)S(1)} %bitcast.7), channel_id=1, source_target_pairs={{0,1},{1,0},{2,3},{3,2},{4,5},{5,4},{6,7},{7,6},{8,9},{9,8},{10,11... | collective-permute-start | bytes 786440 | tf_op jit(solution)/shard_map/ppermute | solution.py:779
  96.1 1.2 %collective-permute-done.5.other = bf16[1024,128]{1,0:T(8,128)(2,1)S(1)} collective-permute-done((bf16[1024,128]{1,0:T(8,128)(2,1)S(1)}, bf16[1024,128]{1,0:T(8,128)(2,1)S(1)}, u32[]{:S(2)}, u32[]{:S(2)}) %collective-permute-start.5) | collective-permute-done | bytes 262176 | tf_op jit(solution)/shard_map/ppermute | solution.py:779
  97.3 1.0 %unpack.1 = (f32[2,2,96]{2,1,0:T(2,128)}, f32[2,96,288]{2,1,0:T(8,128)}, f32[2,288]{1,0:T(2,128)}, f32[3,2,225]{2,1,0:T(2,128)}, f32[2,96,96]{2,1,0:T(8,128)}, /...) custom-call(bf16[1024,128]{1,0:T(8,128)(2,1)S(1)} %bitcast.8, ...), custom_call_target="tpu_custom_call" | custom-call | tf_op jit(solution)/shard_map/unpack/pallas_call | solution.py:780
  (11 shorter events, 0.1 us)
Async XLA Ops:
  0.6 12.6 %copy-start = (bf16[16,48,96]{2,1,0:T(8,128)(2,1)S(1)}, bf16[16,48,96]{2,1,0:T(8,128)(2,1)}, u32[]{:S(2)}) copy-start(bf16[16,48,96]{2,1,0:T(8,128)(2,1)} %rest_1_.1) | copy-start | bytes 442372
  4.8 10.1 %collective-permute-start = (bf16[8,48,96]{2,1,0:T(8,128)(2,1)}, bf16[8,48,96]{2,1,0:T(8,128)(2,1)S(1)}, u32[]{:S(2)}, u32[]{:S(2)}) collective-permute-start(bf16[8,48,96]{2,1,0:T(8,128)(2,1)} %get-tuple-element.47), channel_id=1, source_target_pairs={{0,32},{32,0},{64,96},{96,64},{128,160},{160,128},{192,224},{224,1... | collective-permute-start | bytes 221192 | tf_op jit(solution)/shard_map/ppermute | solution.py:679
  12.6 2.3 %collective-permute-start.1 = (bf16[8,48,96]{2,1,0:T(8,128)(2,1)}, bf16[8,48,96]{2,1,0:T(8,128)(2,1)S(1)}, u32[]{:S(2)}, u32[]{:S(2)}) collective-permute-start(bf16[8,48,96]{2,1,0:T(8,128)(2,1)} %get-tuple-element.48), channel_id=1, source_target_pairs={{32,64},{64,32},{96,128},{128,96},{160,192},{192,160},{33,65},{65,... | collective-permute-start | bytes 221192 | tf_op jit(solution)/shard_map/ppermute | solution.py:678
  13.3 0.9 copy-start.3
  14.9 0.6 copy-start.1
  14.9 0.7 copy-start.2
  15.6 8.4 %collective-permute-start.2 = (bf16[24,8,96]{2,1,0:T(8,128)(2,1)S(1)}, bf16[24,8,96]{2,1,0:T(8,128)(2,1)S(1)}, u32[]{:S(2)}, u32[]{:S(2)}) collective-permute-start(bf16[24,8,96]{2,1,0:T(8,128)(2,1)S(1)} %get-tuple-element.49), channel_id=1, source_target_pairs={{0,1},{1,0},{2,3},{3,2},{4,5},{5,4},{6,7},{7,6},{8,9},{9,8},{10,11... | collective-permute-start | bytes 110600 | tf_op jit(solution)/shard_map/ppermute | solution.py:679
  17.5 6.5 %collective-permute-start.3 = (bf16[24,8,96]{2,1,0:T(8,128)(2,1)S(1)}, bf16[24,8,96]{2,1,0:T(8,128)(2,1)S(1)}, u32[]{:S(2)}, u32[]{:S(2)}) collective-permute-start(bf16[24,8,96]{2,1,0:T(8,128)(2,1)S(1)} %get-tuple-element.50), channel_id=1, source_target_pairs={{1,2},{2,1},{3,4},{4,3},{5,6},{6,5},{7,8},{8,7},{9,10},{10,9},{11,... | collective-permute-start | bytes 110600 | tf_op jit(solution)/shard_map/ppermute | solution.py:678
  24.0 0.6 copy-start.4
  24.0 0.6 copy-start.5
  37.0 1.8 %collective-permute-start.4 = (bf16[1024,128]{1,0:T(8,128)(2,1)}, bf16[1024,128]{1,0:T(8,128)(2,1)S(1)}, u32[]{:S(2)}, u32[]{:S(2)}) collective-permute-start(bf16[1024,128]{1,0:T(8,128)(2,1)} %get-tuple-element.73), channel_id=1, source_target_pairs={{0,1},{1,0},{2,3},{3,2},{4,5},{5,4},{6,7},{7,6},{8,9},{9,8},{10,11... | collective-permute-start | bytes 786440 | tf_op jit(solution)/shard_map/ppermute | solution.py:772
  92.6 4.7 %collective-permute-start.5 = (bf16[1024,128]{1,0:T(8,128)(2,1)S(1)}, bf16[1024,128]{1,0:T(8,128)(2,1)S(1)}, u32[]{:S(2)}, u32[]{:S(2)}) collective-permute-start(bf16[1024,128]{1,0:T(8,128)(2,1)S(1)} %bitcast.7), channel_id=1, source_target_pairs={{0,1},{1,0},{2,3},{3,2},{4,5},{5,4},{6,7},{7,6},{8,9},{9,8},{10,11... | collective-permute-start | bytes 786440 | tf_op jit(solution)/shard_map/ppermute | solution.py:779
